TPU v7x, 32 devices: a whole 2x2x4 slice. The times are simulated.
32 devices in a mesh: frame: 8 (over z, x), space: 4 (over y, core).
Axes of the slice: x: 2, y: 2, z: 4, core: 2. Of those that a mesh axis runs over, the one named last changes fastest.
Arguments:
- queries: bfloat16 [32, 512, 2240], P('frame', 'space'), may hold values from -6 to 6
- keys: bfloat16 [32, 512, 2240], P('frame', 'space'), may hold values from -16 to 16
- values: bfloat16 [32, 512, 2240], P('frame', 'space'), may hold values from -16 to 16
- out_weight: bfloat16 [2240, 2240], P('frame'), may hold values from -0.125 to 0.125
- conv_taps: float32 [3, 2240], replicated, may hold values from -3 to 3
Outputs:
- mixed: bfloat16 [32, 512, 2240], P('frame', 'space')
All inputs are finite; a program needn't handle non-finite values.
Results may differ from a plain program's by a relative error of at most 0.0059.
Values may be sent and summed in bfloat16 or wider, within the bound.
A program may use at most 192 MiB of HBM per device.

v0:
```python
import jax
import jax.numpy as jnp
from jax import lax
from jax.sharding import PartitionSpec as P

HEADS = 20
HEAD_DIM = 112


stab_eps = 1e-06


def prefix(value, axis, join, neutral):
    count, mine = (lax.axis_size(axis), lax.axis_index(axis))
    pieces = jax.tree.map(lambda part: lax.all_gather(part, axis), value)
    subtotal = jax.tree.map(
        lambda part, zero: jnp.full_like(part, 0) + jnp.asarray(zero, part.dtype), value, neutral
    )

    def hop(position, subtotal):
        longer = join(subtotal, jax.tree.map(lambda part: part[position], pieces))
        return jax.tree.map(lambda new, old: jnp.where(position < mine, new, old), longer, subtotal)

    return lax.fori_loop(0, count - 1, hop, subtotal)


def from_behind(block, axis, distance):
    devices = range(lax.axis_size(axis))
    route = [(i - distance, i) for i in devices if i - distance in devices]
    return lax.ppermute(block, axis, route)


def add_states(before_sum, after_sum):
    return (before_sum[0] + after_sum[0], before_sum[1] + after_sum[1])


def per_device(queries, keys, values, out_weight, conv_taps):
    frame_count = queries.shape[0]
    spatial_count = queries.shape[1]
    model_width = queries.shape[2]
    key_relu = jax.nn.relu(keys).reshape(frame_count, spatial_count, HEADS, HEAD_DIM)
    value_rows = values.reshape(frame_count, spatial_count, HEADS, HEAD_DIM)
    key_value = jnp.einsum(
        "fshd,fshe->fhde", key_relu, value_rows, preferred_element_type=jnp.float32
    )
    key_sums = jnp.sum(key_relu, axis=1, dtype=jnp.float32)
    frame_kv, frame_ksum = lax.psum((key_value, key_sums), "space")
    section_total = (jnp.sum(frame_kv, axis=0), jnp.sum(frame_ksum, axis=0))
    empty_state = (jnp.zeros_like(section_total[0]), jnp.zeros_like(section_total[1]))
    prefix_kv, prefix_ks = prefix(section_total, "frame", add_states, empty_state)
    states = prefix_kv[None] + jnp.cumsum(frame_kv, axis=0)
    norms = prefix_ks[None] + jnp.cumsum(frame_ksum, axis=0)
    query_relu = jax.nn.relu(queries).reshape(frame_count, spatial_count, HEADS, HEAD_DIM)
    numerator = jnp.einsum(
        "fshd,fhde->fshe",
        query_relu,
        states,
        precision=lax.Precision.HIGHEST,
        preferred_element_type=jnp.float32,
    )
    denominator = (
        jnp.einsum(
            "fshd,fhd->fsh",
            query_relu,
            norms,
            precision=lax.Precision.HIGHEST,
            preferred_element_type=jnp.float32,
        )
        + stab_eps
    )
    attention = (
        (numerator / denominator[..., None])
        .reshape(frame_count * spatial_count, model_width)
        .astype(jnp.bfloat16)
    )
    projected = jnp.dot(
        attention,
        lax.all_gather(out_weight, "frame", axis=0, tiled=True),
        preferred_element_type=jnp.float32,
    )
    projected = projected.astype(jnp.bfloat16).reshape(frame_count, spatial_count, model_width)
    earlier_frames = from_behind(projected[frame_count - 2 :], "frame", 1)
    extended = jnp.concatenate([earlier_frames, projected], axis=0)
    mixed_out = (
        conv_taps[0] * extended[2:] + conv_taps[1] * extended[1:-1] + conv_taps[2] * extended[:-2]
    )
    return mixed_out.astype(jnp.bfloat16)


def solution(mesh):
    in_specs = (
        P("frame", "space", None),
        P("frame", "space", None),
        P("frame", "space", None),
        P("frame", None),
        P(),
    )
    out_specs = P("frame", "space", None)
    return jax.shard_map(
        per_device, mesh=mesh, in_specs=in_specs, out_specs=out_specs, check_vma=False
    )
```

profile of v0, /device:TPU:31, one launch (start us, length us, event | category | flops | bytes accessed | tf_op | source)
XLA Modules:
  0.0 439.2 jit_solution(14089704421223579940)
XLA Ops:
  6.5 1.9 broadcast_maximum_fusion.1
  8.9 3.4 fusion.13
  12.3 92.3 %all-reduce.2.cloned.1.call-done = f32[4,20,112,112]{3,2,1,0:T(8,128)} async-done(((f32[4,20,112,112]{3,2,1,0:T(8,128)}), f32[4,20,112,112]{3,2,1,0:T(8,128)}) %all-reduce.2.cloned.1.call-update) | async-done | bytes 4014096 | tf_op jit(solution)/shard_map/psum | solution.py:47
  104.7 3.8 reduce_sum.29
  109.2 2.4 convert_reduce_fusion
  111.7 10.9 %psum.15 = f32[4,20,112]{2,1,0:T(8,128)S(1)} all-reduce(f32[4,20,112]{2,1,0:T(8,128)S(1)} %reduce_sum.31), channel_id=1, replica_groups=mesh['frame'=8,'space'=4] {'space'}, use_global_device_ids=true, to_apply=%region_3.4 | all-reduce | flops 8960 | bytes 71680 | tf_op jit(solution)/shard_map/psum | solution.py:47
  122.6 27.3 %all-gather.2 = f32[8,20,112]{2,1,0:T(8,128)} all-gather(f32[1,20,112]{2,1,0:T(8,128)S(1)} %bitcast.58), channel_id=3, replica_groups=mesh['frame'=8,'space'=4] {'frame'}, dimensions={0}, use_global_device_ids=true | all-gather | bytes 80640 | tf_op jit(solution)/shard_map/all_gather | solution.py:15
  149.9 3.3 broadcast_maximum_fusion
  153.3 2.5 fusion.12
  155.7 86.6 %all-gather.8.cloned.1.call-done = f32[160,112,112]{2,1,0:T(8,128)} async-done(((f32[20,112,112]{2,1,0:T(8,128)}), f32[160,112,112]{2,1,0:T(8,128)}) %all-gather.8.cloned.1.call-update) | async-done | bytes 8028176 | tf_op jit(solution)/shard_map/all_gather | solution.py:15
  242.3 16.4 %while.16 = (s32[]{:T(128)}, f32[20,112,112]{2,1,0:T(8,128)S(1)}, f32[20,112]{1,0:T(8,128)S(1)}, s32[]{:T(128)}, f32[8,20,112,112]{3,2,1,0:T(8,128)}, /*index=5*/f32[8,20,112]{2,1,0:T(8,128)}, s32[]{:T(128)}, s32[]{:T(128)}) while((s32[]{:T(128)}, f32[20,112,112]{2,1,0:T(8,128)S(1)}, f32[20,112]{1,0:T(8,128)S(1)}, s32[]{:T(128)}, ...), condition=%wide.region_6.7_spmd.clone, body=%wide.region_5.6_spmd.clone.sunk | while | flops 759364 | bytes 3037555 | solution.py:24
  242.3 1.6 add_select_fusion.4
  243.9 0.7 add_select_fusion.5
  244.6 1.6 add_select_fusion.4
  246.2 0.7 add_select_fusion.5
  247.0 1.6 add_select_fusion.4
  248.6 0.7 add_select_fusion.5
  249.3 1.6 add_select_fusion.4
  250.9 0.7 add_select_fusion.5
  251.6 1.6 add_select_fusion.4
  253.2 0.7 add_select_fusion.5
  253.9 1.8 add_select_fusion.4
  255.7 0.7 add_select_fusion.5
  256.4 1.6 add_select_fusion.4
  258.8 3.7 fusion.10
  262.5 6.2 %fusion = bf16[4,128,20,112]{1,3,2,0:T(8,128)(2,1)S(1)} fusion(f32[4,128,20]{1,2,0:T(8,128)S(1)} %fusion.9, bf16[4,128,20,112]{1,3,2,0:T(8,128)(2,1)S(1)} %bitcast.55, f32[4,20,112,112]{3,2,1,0:T(8,128)} %fusion.12, f32[20,112,112]{2,1,0:T(8,128)S(1)} %get-tuple-element.115), kind=kOutput, calls=%fused_computation.3 | convolution fusion | flops 1544704000 | bytes 9646080 | tf_op jit(solution)/shard_map/fshd,fhde->fshe/dot_general | solution.py:54
  268.7 3.2 copy.16
  271.9 119.7 %all-gather.6.cloned.1.call-done = bf16[2240,2240]{1,0:T(8,128)(2,1)} async-done(((bf16[280,2240]{1,0:T(8,128)(2,1)}), bf16[2240,2240]{1,0:T(8,128)(2,1)}) %all-gather.6.cloned.1.call-update) | async-done | bytes 10035216 | tf_op jit(solution)/shard_map/all_gather | solution.py:78
  391.6 9.1 %convolution_convert_fusion = bf16[512,2240]{0,1:T(8,128)(2,1)S(1)} fusion(bf16[2240,2240]{1,0:T(8,128)(2,1)} %all-gather.6.cloned.1.call-done, bf16[280,8,4,128]{3,2,1,0:T(4,128)(2,1)} %bitcast.57), kind=kOutput, calls=%fused_computation.8 | convolution fusion | flops 5139169280 | bytes 14622720 | tf_op jit(solution)/shard_map/dot_general | solution.py:76
  400.8 1.3 collective-permute-start
  402.2 26.9 %collective-permute-done = bf16[2,128,2240]{1,2,0:T(8,128)(2,1)S(1)} collective-permute-done((bf16[2,128,2240]{1,2,0:T(8,128)(2,1)S(1)}, bf16[2,128,2240]{1,2,0:T(8,128)(2,1)S(1)}, u32[]{:S(2)}, u32[]{:S(2)}) %collective-permute-start) | collective-permute-done | bytes 1146912 | tf_op jit(solution)/shard_map/ppermute | solution.py:30
  429.8 2.9 add_convert_fusion
  (25 shorter events, 2.8 us)
Async XLA Ops:
  6.5 2.3 copy-start
  6.5 98.1 %all-reduce.2.cloned.1.call-start = ((), (), s32[]{:S(2)}) async-start(), calls=%async_computation | async-start | bytes 9175040 | tf_op jit(solution)/shard_map/psum | solution.py:47
  12.3 230.0 %all-gather.8.cloned.1.call-start = ((), (), s32[]{:S(2)}) async-start(), calls=%async_computation.2 | async-start | bytes 10321920 | tf_op jit(solution)/shard_map/all_gather | solution.py:15
  108.4 283.1 %all-gather.6.cloned.1.call-start = ((), (), s32[]{:S(2)}) async-start(), calls=%async_computation.1 | async-start | bytes 11612160 | tf_op jit(solution)/shard_map/all_gather | solution.py:78
  149.9 3.3 copy-start.1
  258.8 3.7 copy-start.2
  400.7 1.4 copy-start.3
  400.8 28.3 %collective-permute-start = (bf16[2,128,2240]{1,2,0:T(8,128)(2,1)S(1)}, bf16[2,128,2240]{1,2,0:T(8,128)(2,1)S(1)}, u32[]{:S(2)}, u32[]{:S(2)}) collective-permute-start(bf16[2,128,2240]{1,2,0:T(8,128)(2,1)S(1)} %copy_bitcast_fusion), channel_id=1, source_target_pairs={{0,4},{4,8},{8,12},{12,16},{16,20},{20,24},{24,28},{1,5},{5,9},{9,... | collective-permute-start | bytes 3440648 | tf_op jit(solution)/shard_map/ppermute | solution.py:30
Sparse Core Ops, SparseCore 0:
  12.4 92.1 all-reduce.1
  108.6 133.7 all-gather.7
  244.5 147.0 all-gather.5
where the time goes:
time: 443 us; the launch traced here: 439 us
  waiting for transfers between devices  326 us (74%)
  blocking collectives  38.2 us (9%)
  other arithmetic  33.2 us (7%)
  matrix products  22.5 us (5%)
  between operations  13.2 us (3%)
    all_gather x1, waiting for transfers between devices, per_device(): lax.all_gather(out_weight, 'frame', axis=0, tiled=True)  120 us
    psum x1, waiting for transfers between devices, per_device(): frame_kv, frame_ksum = lax.psum((key_value, key_sums), 'space')  92.3 us
    all_gather x1, waiting for transfers between devices, prefix(): pieces = jax.tree.map(lambda part: lax.all_gather(part, axis), value)  86.6 us
    all_gather x1, blocking collectives, prefix(): pieces = jax.tree.map(lambda part: lax.all_gather(part, axis), value)  27.3 us
    ppermute x1, waiting for transfers between devices, from_behind(): return lax.ppermute(block, axis, route)  26.9 us
    select_n x14, other arithmetic, hop(): jnp.where(position < mine, new, old)  16.4 us
    psum x1, blocking collectives, per_device(): frame_kv, frame_ksum = lax.psum((key_value, key_sums), 'space')  10.9 us
    dot_general x1, matrix products, per_device(): jnp.dot(attention, lax.all_gather(out_weight, 'frame', axis=0, tiled=True...  9.15 us
  transfers between devices with their start and end apart: 4, of which 4 were waited for; matrix products, arithmetic and copies ran while one was open for 9% of the time, Pallas kernels for 0%

commit v1 on v0

v1 whole, which is shorter than its diff:
```python
import functools

import jax
import jax.numpy as jnp
from jax import lax
from jax.experimental import pallas as pl
from jax.experimental.pallas import tpu as pltpu
from jax.sharding import PartitionSpec as P

HEADS = 20
HEAD_DIM = 112
LANES = 128
HALO = 2
stab_eps = 1e-06
MESH = pl.DeviceIdType.MESH


def exchange(outer, lanes_y, kv_in, w_in, q_in, st_out, w_out, q_out,
             sib_kv, chip_kv, y_kv, frame_kv, x_got, pair_msg, edge_msg, pair_got, edge_got,
             own_sem, kv_sem, z_sem, x_sem, y_sem, sz_sem, sx_sem, sy_sem, p_sem):
    frame = lax.axis_index("frame")
    space = lax.axis_index("space")
    o, i = frame // 2, frame % 2
    y, c = space // 2, space % 2
    frames = kv_in.shape[2]
    rows = w_in.shape[1]
    part = rows // lanes_y

    def at(o_=None, i_=None, y_=None, c_=None):
        o_ = o if o_ is None else o_
        i_ = i if i_ is None else i_
        y_ = y if y_ is None else y_
        c_ = c if c_ is None else c_
        return (o_ * 2 + i_, y_ * 2 + c_)

    def copy(src, dst, sems, to):
        return pltpu.make_async_remote_copy(
            src_ref=src, dst_ref=dst, send_sem=sems.at[0], recv_sem=sems.at[1],
            device_id=to, device_id_type=MESH)

    def when(cond, do):
        if cond is True:
            do()
        else:
            pl.when(cond)(do)

    def y_far(d):
        return lax.rem(y + d, lanes_y)

    def y_from(d):
        return lax.rem(y + lanes_y - d, lanes_y)

    barrier = pltpu.get_barrier_semaphore()

    def greet(to):
        pl.semaphore_signal(barrier, inc=1, device_id=to, device_id_type=MESH)

    for d in range(1, outer):
        greet(at(o_=lax.rem(o + d, outer)))
    for d in range(1, lanes_y):
        greet(at(y_=y_far(d)))
    greet(at(i_=1 - i))
    greet(at(c_=1 - c))
    into = jnp.logical_and(i == 0, o > 0)
    onto = jnp.logical_and(i == 1, o < outer - 1)
    when(into, lambda: greet(at(o_=o - 1, i_=1)))
    when(onto, lambda: greet(at(o_=o + 1, i_=0)))
    peers = (outer - 1) + (lanes_y - 1) + 2
    pl.semaphore_wait(barrier, peers + jnp.where(jnp.logical_or(into, onto), 1, 0))

    def source(key):
        t = (key + 1) // 2
        if key == 0:
            return o, True
        if key % 2:
            return o - t, o >= t
        return o + t, o + t < outer

    keys = range(2 * outer - 1)
    sent = []

    def launch(cond, make):
        when(cond, lambda: make().start())
        sent.append((cond, make))

    def mine(key):
        return w_out.at[c, source(key)[0] * 2 + i]

    def theirs(key, y_):
        span = pl.ds(pl.multiple_of(y_ * part, 16), part)
        return w_out.at[c, source(key)[0] * 2 + 1 - i, span]

    def z_copy(up, t):
        g = ((o - t + 1) if up else (o + t - 1)) * 2 + i
        dst = w_out.at[c, g]
        return copy(w_in.at[c] if t == 1 else dst, dst, z_sem.at[0 if up else 1, t],
                    at(o_=o + 1 if up else o - 1))

    def z_send(t):
        launch(jnp.logical_and(o < outer - 1, o - t + 1 >= 0), lambda: z_copy(True, t))
        launch(jnp.logical_and(o > 0, o + t - 1 < outer), lambda: z_copy(False, t))

    def z_wait(t):
        def got(key, up):
            ref = mine(key)
            copy(ref, ref, z_sem.at[0 if up else 1, t], at(c_=1 - c)).wait_recv()
        when(source(2 * t - 1)[1], lambda: got(2 * t - 1, True))
        when(source(2 * t)[1], lambda: got(2 * t, False))

    def x_copy(key):
        span = pl.ds(pl.multiple_of(y * part, 16), part)
        src = w_in.at[c, span] if key == 0 else mine(key).at[span]
        return copy(src, mine(key).at[span], x_sem.at[key], at(i_=1 - i))

    def x_send(key):
        launch(source(key)[1], lambda: x_copy(key))

    def sib_z(key):
        launch(source(key)[1], lambda: copy(mine(key), mine(key), sz_sem.at[key], at(c_=1 - c)))

    def x_pass(key):
        def got():
            ref = theirs(key, y)
            copy(ref, ref, x_sem.at[key], at(i_=1 - i)).wait_recv()
        cond = source(key)[1]
        when(cond, got)
        for d in range(1, lanes_y):
            launch(cond, lambda d=d: copy(theirs(key, y), theirs(key, y), y_sem.at[key, d],
                                          at(y_=y_far(d))))
        launch(cond, lambda: copy(theirs(key, y), theirs(key, y), sx_sem.at[key], at(c_=1 - c)))

    def y_pass(key):
        cond = source(key)[1]
        for d in range(1, lanes_y):
            def got(d=d):
                ref = theirs(key, y_from(d))
                copy(ref, ref, y_sem.at[key, d], at(y_=y_far(d))).wait_recv()
            when(cond, got)
            launch(cond, lambda d=d: copy(theirs(key, y_from(d)), theirs(key, y_from(d)),
                                          sy_sem.at[key, d], at(c_=1 - c)))

    def sib_wait(key):
        cond = source(key)[1]
        g = source(key)[0] * 2

        def got(ref, sems):
            copy(ref, ref, sems, at(c_=1 - c)).wait_recv()
        if key:
            when(cond, lambda: got(w_out.at[1 - c, g + i], sz_sem.at[key]))
        for d in range(lanes_y):
            span = pl.ds(pl.multiple_of(y_from(d) * part, 16), part)
            sems = sx_sem.at[key] if d == 0 else sy_sem.at[key, d]
            when(cond, lambda span=span, sems=sems: got(w_out.at[1 - c, g + 1 - i, span], sems))

    sib_copy = copy(kv_in.at[1 - c], sib_kv, kv_sem.at[0], at(c_=1 - c))
    sib_copy.start()
    z_send(1)
    x_send(0)
    own = pltpu.make_async_copy(w_in, w_out.at[:, frame], own_sem.at[0])
    own.start()
    last = q_in.at[pl.ds(frames - HALO, HALO)]
    q_next = lambda: copy(last, q_out, p_sem.at[0], (frame + 1, space))
    launch(frame < 2 * outer - 1, q_next)

    sib_copy.wait_recv()
    for y_ in range(lanes_y):
        for f in range(frames):
            chip_kv[y_, f] = (kv_in[c, y_, f].astype(jnp.float32)
                              + sib_kv[y_, f].astype(jnp.float32)).astype(jnp.bfloat16)
    for d in range(1, lanes_y):
        launch(True, lambda d=d: copy(chip_kv.at[y_far(d)], y_kv.at[d], kv_sem.at[1 + d],
                                      at(y_=y_far(d))))
    x_pass(0)
    for d in range(1, lanes_y):
        copy(chip_kv.at[y_far(d)], y_kv.at[d], kv_sem.at[1 + d], at(y_=y_far(d))).wait_recv()
    for f in range(frames):
        total = chip_kv[y, f].astype(jnp.float32)
        for d in range(1, lanes_y):
            total = total + y_kv[d, f].astype(jnp.float32)
        frame_kv[f] = total if f == 0 else frame_kv[f - 1] + total
    for f in range(HALO):
        x_got[0, f] = frame_kv[frames - 1 - f].astype(jnp.bfloat16)
    launch(True, lambda: copy(x_got.at[0], x_got.at[1], p_sem.at[1], at(i_=1 - i)))

    z_wait(1)
    if outer > 2:
        z_send(2)
    for key in (1, 2):
        x_send(key)
        sib_z(key)

    copy(x_got.at[0], x_got.at[1], p_sem.at[1], at(i_=1 - i)).wait_recv()
    pair_msg[...] = (x_got[0, 0].astype(jnp.float32) + x_got[1, 0].astype(jnp.float32)).astype(jnp.bfloat16)
    low = jnp.where(i == 0, x_got[0, 0], x_got[1, 0]).astype(jnp.float32)
    high = jnp.where(i == 0, x_got[1, 1], x_got[0, 1]).astype(jnp.float32)
    edge_msg[...] = (low + high).astype(jnp.bfloat16)
    for d in range(1, outer):
        launch(o + d < outer, lambda d=d: copy(pair_msg, pair_got.at[d], p_sem.at[3 + d], at(o_=o + d)))
    launch(o + 1 < outer, lambda: copy(edge_msg, edge_got, p_sem.at[2], at(o_=o + 1)))

    y_pass(0)
    for key in (1, 2):
        x_pass(key)

    for d in range(1, outer):
        when(o >= d, lambda d=d: copy(pair_msg, pair_got.at[d], p_sem.at[3 + d], at(c_=1 - c)).wait_recv())
    when(o >= 1, lambda: copy(edge_msg, edge_got, p_sem.at[2], at(c_=1 - c)).wait_recv())
    zero = jnp.zeros(pair_msg.shape, jnp.float32)
    far = zero
    for d in range(2, outer):
        far = far + jnp.where(o >= d, pair_got[d].astype(jnp.float32), zero)
    near = jnp.where(o >= 1, pair_got[1].astype(jnp.float32), zero)
    edge = jnp.where(o >= 1, edge_got[...].astype(jnp.float32), zero)
    base = far + near
    before = jnp.where(i == 0, base, base + x_got[1, 0].astype(jnp.float32))
    second = jnp.where(i == 0, far + edge, base + x_got[1, 1].astype(jnp.float32))
    st_out[c, y, 0] = second.astype(jnp.bfloat16)
    st_out[c, y, 1] = before.astype(jnp.bfloat16)
    for f in range(frames):
        st_out[c, y, HALO + f] = (before + frame_kv[f]).astype(jnp.bfloat16)
    for d in range(1, lanes_y):
        launch(True, lambda d=d: copy(st_out.at[c, y], st_out.at[c, y], kv_sem.at[lanes_y + d],
                                      at(y_=y_far(d))))

    for t in range(2, outer):
        z_wait(t)
        if t + 1 < outer:
            z_send(t + 1)
        for key in (2 * t - 1, 2 * t):
            x_send(key)
            sib_z(key)
        for key in (2 * t - 3, 2 * t - 2):
            y_pass(key)
        if t == 2:
            for d in range(1, lanes_y):
                ref = st_out.at[c, y_from(d)]
                copy(ref, ref, kv_sem.at[lanes_y + d], at(y_=y_far(d))).wait_recv()
            launch(True, lambda: copy(st_out.at[c], st_out.at[c], kv_sem.at[1], at(c_=1 - c)))
        for key in (2 * t - 1, 2 * t):
            x_pass(key)
    for key in (2 * outer - 3, 2 * outer - 2):
        y_pass(key)

    other = st_out.at[1 - c]
    copy(other, other, kv_sem.at[1], at(c_=1 - c)).wait_recv()
    when(frame > 0, lambda: copy(last, q_out, p_sem.at[0], at(c_=1 - c)).wait_recv())
    for key in keys:
        sib_wait(key)
    own.wait()
    sib_copy.wait_send()
    for cond, make in sent:
        when(cond, lambda make=make: make().wait_send())


def exchanged(kv, weight, queries, outer, lanes_y):
    rows = kv.shape[3]
    frames = kv.shape[2]
    keys = 2 * outer - 1
    tile = (rows, LANES)
    half = jnp.bfloat16
    dma = pltpu.SemaphoreType.DMA
    whole = pl.BlockSpec(memory_space=pltpu.VMEM)
    anywhere = pl.BlockSpec(memory_space=pl.ANY)
    return pl.pallas_call(
        functools.partial(exchange, outer, lanes_y),
        out_shape=(
            jax.ShapeDtypeStruct((2, lanes_y, HALO + frames) + tile, half),
            jax.ShapeDtypeStruct((2, 2 * outer) + weight.shape[1:], half),
            jax.ShapeDtypeStruct((HALO,) + queries.shape[1:], half),
        ),
        in_specs=[whole, anywhere, anywhere],
        out_specs=(whole, anywhere, anywhere),
        scratch_shapes=[
            pltpu.VMEM((lanes_y, frames) + tile, half),
            pltpu.VMEM((lanes_y, frames) + tile, half),
            pltpu.VMEM((lanes_y, frames) + tile, half),
            pltpu.VMEM((frames,) + tile, jnp.float32),
            pltpu.VMEM((2, HALO) + tile, half),
            pltpu.VMEM(tile, half),
            pltpu.VMEM(tile, half),
            pltpu.VMEM((outer,) + tile, half),
            pltpu.VMEM(tile, half),
            dma((1,)),
            dma((2 * lanes_y, 2)),
            dma((2, outer, 2)),
            dma((keys, 2)),
            dma((keys, lanes_y, 2)),
            dma((keys, 2)),
            dma((keys, 2)),
            dma((keys, lanes_y, 2)),
            dma((3 + outer, 2)),
        ],
        compiler_params=pltpu.CompilerParams(
            collective_id=0, has_side_effects=True, vmem_limit_bytes=40 * 2**20),
    )(kv, weight, queries)


def up_to(value, multiple):
    return -(-value // multiple) * multiple


def per_device(sections, lanes, queries, keys, values, out_weight, conv_taps):
    frames, tokens, width = queries.shape
    lanes_y = lanes // 2
    outer = sections // 2
    key_relu = jax.nn.relu(keys).reshape(frames, tokens, HEADS, HEAD_DIM)
    rows = values.reshape(frames, tokens, HEADS, HEAD_DIM)
    ones = jnp.ones((frames, tokens, HEADS, 1), rows.dtype)
    rows = jnp.pad(jnp.concatenate([rows, ones], axis=3), ((0, 0), (0, 0), (0, 0), (0, LANES - HEAD_DIM - 1)))
    kv = jnp.einsum("fshd,fshe->fhde", key_relu, rows, preferred_element_type=jnp.float32)
    kv = kv.astype(jnp.bfloat16).reshape(frames, width, LANES)
    tall = up_to(width, 16 * lanes)
    kv = jnp.pad(kv, ((0, 0), (0, tall - width), (0, 0)))
    kv = kv.reshape(frames, 2, lanes_y, tall // lanes, LANES).transpose(1, 2, 0, 3, 4)
    deep = out_weight.shape[0]
    deep_pad = up_to(deep, 16 * lanes_y)
    wide = up_to(width, 2 * LANES)
    weight = jnp.pad(out_weight, ((0, deep_pad - deep), (0, wide - width)))
    weight = weight.reshape(deep_pad, 2, wide // 2).transpose(1, 0, 2)
    states, weight, earlier = exchanged(kv, weight, queries, outer, lanes_y)
    states = states.transpose(2, 0, 1, 3, 4).reshape(HALO + frames, tall, LANES)[:, :width]
    states = states.reshape(HALO + frames, HEADS, HEAD_DIM, LANES)
    first = lax.axis_index("frame") == 0
    earlier = jnp.where(first, jnp.zeros_like(earlier), earlier)
    query_relu = jax.nn.relu(jnp.concatenate([earlier, queries], axis=0))
    query_relu = query_relu.reshape(HALO + frames, tokens, HEADS, HEAD_DIM)
    sums = jnp.einsum("fshd,fhde->fshe", query_relu, states, preferred_element_type=jnp.float32)
    attention = sums[..., :HEAD_DIM] / (sums[..., HEAD_DIM:HEAD_DIM + 1] + stab_eps)
    attention = attention.astype(jnp.bfloat16).reshape((HALO + frames) * tokens, sections, deep)
    attention = jnp.pad(attention, ((0, 0), (0, 0), (0, deep_pad - deep)))
    attention = attention.reshape((HALO + frames) * tokens, sections * deep_pad)
    weight = weight.reshape(2, sections * deep_pad, wide // 2)
    projected = jnp.concatenate(
        [jnp.dot(attention, weight[n], preferred_element_type=jnp.float32).astype(jnp.bfloat16)
         for n in range(2)], axis=1)[:, :width]
    extended = projected.reshape(HALO + frames, tokens, width)
    mixed = conv_taps[0] * extended[2:] + conv_taps[1] * extended[1:-1] + conv_taps[2] * extended[:-2]
    return mixed.astype(jnp.bfloat16)


def solution(mesh):
    split = P("frame", "space", None)
    return jax.shard_map(
        functools.partial(per_device, mesh.shape["frame"], mesh.shape["space"]), mesh=mesh,
        in_specs=(split, split, split, P("frame", None), P()), out_specs=split, check_vma=False)
```

time: 443 us -> 194 us (0.44)
  waiting for transfers between devices: 326 us -> 0 us
  Pallas kernels: 0 us -> 108 us
  local copies, waits for them, and re-layouts: 4.42 us -> 50.5 us
  blocking collectives: 38.2 us -> 0 us
  other arithmetic: 33.2 us -> 17.5 us
  between operations: 13.2 us -> 0.13 us
  matrix products: 22.5 us -> 17 us
    all_gather x2 -> x0, waiting for transfers between devices: 206 us -> none  [the longest x1 120 us: per_device(): lax.all_gather(out_weight, 'frame', axis=0, tiled=True)]
    pallas_call x0 -> x1, Pallas kernels: none -> 108 us  [exchanged(): pl.pallas_call(functools.partial(exchange, outer, lanes_y), out_shape=(ja...]
    psum x1 -> x0, waiting for transfers between devices: 92.3 us -> none  [per_device(): frame_kv, frame_ksum = lax.psum((key_value, key_sums), 'space')]
    all_gather x1 -> x0, blocking collectives: 27.3 us -> none  [prefix(): pieces = jax.tree.map(lambda part: lax.all_gather(part, axis), value)]
    ppermute x1 -> x0, waiting for transfers between devices: 26.9 us -> none  [from_behind(): return lax.ppermute(block, axis, route)]
    select_n x14 -> x1, other arithmetic: 16.4 us -> 1.09 us  [per_device(): earlier = jnp.where(first, jnp.zeros_like(earlier), earlier)]
    convert_element_type x1 -> x4, local copies, waits for them, and re-layouts: 3.16 us -> 16.6 us  [the longest x1 4.55 us: per_device(): conv_taps[1] * extended[1:-1]]
    reshape x0 -> x4, local copies, waits for them, and re-layouts: none -> 12.9 us  [the longest x1 7.01 us: per_device(): attention.astype(jnp.bfloat16)]
  transfers between devices with their start and end apart: 4 -> 0, of which waited for: 4 -> 0; matrix products, arithmetic and copies ran while one was open for 9% -> 0% of each run, Pallas kernels for 0% -> 0%
where the time goes in v1:
time: 194 us; the launch traced here: 193 us
  Pallas kernels  108 us (56%)
  local copies, waits for them, and re-layouts  50.5 us (26%)
  other arithmetic  17.5 us (9%)
  matrix products  17 us (9%)
    pallas_call x1, Pallas kernels, exchanged(): pl.pallas_call(functools.partial(exchange, outer, lanes_y), out_shape=(ja...  108 us
    dot_general x2, matrix products, per_device(): jnp.dot(attention, weight[n], preferred_element_type=jnp.float32)  12.3 us
    slice x1, local copies, waits for them, and re-layouts, per_device(): weight[n]  8.9 us
    convert_element_type x1, other arithmetic, per_device(): return mixed.astype(jnp.bfloat16)  7.18 us
    reshape x1, local copies, waits for them, and re-layouts, per_device(): attention.astype(jnp.bfloat16)  7.01 us
    concatenate x1, other arithmetic, per_device(): jnp.concatenate([jnp.dot(attention, weight[n], preferred_element_type=jnp...  6.4 us
    unnamed x16, local copies, waits for them, and re-layouts  6.09 us
    convert_element_type x1, local copies, waits for them, and re-layouts, per_device(): conv_taps[1] * extended[1:-1]  4.55 us

profile of v1, /device:TPU:31, one launch (start us, length us, event | category | flops | bytes accessed | tf_op | source)
XLA Modules:
  0.0 193.1 jit_solution(17285350478715875095)
XLA Ops:
  0.0 3.2 %copy.11 = bf16[4,128,20,112]{3,1,2,0:T(8,128)(2,1)S(1)} copy(bf16[4,128,20,112]{1,3,2,0:T(8,128)(2,1)} %bitcast.53) | data formatting | bytes 4587520 | tf_op jit(solution)/shard_map/reshape | solution.py:307
  3.2 1.8 broadcast_maximum_fusion
  5.0 1.3 fusion.12
  6.3 0.0 copy-start.5
  6.3 1.5 copy.26
  7.9 0.3 copy-done.5
  8.2 0.1 pad.14
  8.3 1.2 copy.27
  9.4 2.8 %copy.14.q_in = bf16[4,128,2240]{2,1,0:T(8,128)(2,1)S(1)} copy(bf16[4,128,2240]{1,2,0:T(8,128)(2,1)} %param.5) | data formatting | bytes 4587520 | tf_op args[0]
  12.3 0.0 copy-start
  12.3 1.6 copy-done
  13.9 1.3 copy-done.1
  15.2 107.9 %shard_map.55 = (bf16[2,2,6,560,128]{4,3,2,1,0:T(8,128)(2,1)S(1)}, bf16[2,8,288,1152]{3,2,1,0:T(8,128)(2,1)}, bf16[2,128,2240]{2,1,0:T(8,128)(2,1)S(1)}) custom-call(bf16[2,2,4,560,128]{4,3,2,1,0:T(8,128)(2,1)S(1)} %bitcast.39, bf16[2,288,1152]{2,1,0:T(8,128)(2,1)S(1)} %bitcast.40, bf16[4,128,2240]{2,1,0:T(8,128)(2,1)S(1)} %copy.14.q_in), custom_call_target="tpu_custom_call" | custom-call | tf_op jit(solution)/shard_map/pallas_call | solution.py:264
  123.2 2.1 %copy.15 = bf16[6,2,2,560,128]{4,3,2,1,0:T(8,128)(2,1)} copy(bf16[6,2,2,560,128]{4,3,0,2,1:T(8,128)(2,1)S(1)} %bitcast.41) | data formatting | bytes 6881280 | tf_op jit(solution)/shard_map/transpose | solution.py:321
  125.3 1.1 broadcast_select_fusion
  126.4 1.7 copy.16
  128.1 0.0 copy-done.2
  128.2 3.3 %fusion.5 = f32[6,128,20,128]{1,3,2,0:T(8,128)S(1)} fusion(bf16[6,20,112,128]{3,2,1,0:T(8,128)(2,1)} %bitcast.42, bf16[4,128,20,112]{1,3,2,0:T(8,128)(2,1)S(1)} %bitcast.46, bf16[2,128,20,112]{1,3,2,0:T(8,128)(2,1)S(1)} %bitcast.50), kind=kOutput, calls=%fused_computation.15 | convolution fusion | flops 443842560 | bytes 14745600 | tf_op jit(solution)/shard_map/fshd,fhde->fshe/dot_general | solution.py:327
  131.5 0.1 slice_add_fusion
  131.6 1.0 fusion
  132.6 4.5 %copy.17 = bf16[6,128,20,112]{1,0,3,2:T(8,128)(2,1)} copy(bf16[6,128,20,112]{1,3,2,0:T(8,128)(2,1)S(1)} %fusion) | data formatting | bytes 6881280 | tf_op jit(solution)/shard_map/convert_element_type | solution.py:329
  137.1 7.0 %reshape.45 = bf16[768,8,280]{0,2,1:T(8,128)(2,1)S(1)} reshape(bf16[6,128,20,112]{1,0,3,2:T(8,128)(2,1)} %copy.17) | data formatting | bytes 6881280 | tf_op jit(solution)/shard_map/reshape | solution.py:329
  144.2 2.0 %pad.15 = bf16[768,8,288]{0,2,1:T(8,128)(2,1)} pad(bf16[768,8,280]{0,2,1:T(8,128)(2,1)S(1)} %reshape.45, bf16[]{:T(256)} %constant.6.clone.1), padding=0_0x0_0x0_8 | pad | bytes 6979586 | tf_op jit(solution)/shard_map/jit(_pad)/pad | solution.py:330
  146.2 8.9 %fusion.22 = (bf16[1,8,288,1152]{3,2,1,0:T(8,128)(2,1)}, bf16[1,8,288,1152]{3,2,1,0:T(8,128)(2,1)}) fusion(bf16[2,8,288,1152]{3,2,1,0:T(8,128)(2,1)} %get-tuple-element.10), kind=kLoop, calls=%fused_computation.39 | loop fusion | bytes 21233664 | tf_op jit(solution)/shard_map/slice | solution.py:334
  155.1 7.5 %convolution_convert_fusion = bf16[768,1152]{1,0:T(8,128)(2,1)S(1)} fusion(bf16[768,2304]{0,1:T(8,128)(2,1)S(1)} %bitcast.51, bf16[2304,1152]{1,0:T(8,128)(2,1)} %bitcast.49), kind=kOutput, calls=%fused_computation.13 | convolution fusion | flops 4077748224 | bytes 10616832 | tf_op jit(solution)/shard_map/dot_general | solution.py:334
  162.5 4.8 %convolution_convert_fusion.1 = bf16[768,1152]{1,0:T(8,128)(2,1)S(1)} fusion(bf16[768,2304]{0,1:T(8,128)(2,1)S(1)} %bitcast.52, bf16[2304,1152]{1,0:T(8,128)(2,1)S(1)} %bitcast.48), kind=kOutput, calls=%fused_computation.14 | convolution fusion | flops 4077748224 | bytes 10616832 | tf_op jit(solution)/shard_map/dot_general | solution.py:334
  167.4 6.4 %fusion.11 = (bf16[512,2240]{1,0:T(8,128)(2,1)}, bf16[512,2240]{1,0:T(8,128)(2,1)S(1)}, bf16[512,2240]{1,0:T(8,128)(2,1)}) fusion(bf16[768,1152]{1,0:T(8,128)(2,1)S(1)} %convolution_convert_fusion.1, bf16[768,1152]{1,0:T(8,128)(2,1)S(1)} %convolution_convert_fusion), kind=kLoop, calls=%fused_computation.20 | loop fusion | flops 13762560 | bytes 10420224 | tf_op jit(solution)/shard_map/concatenate | solution.py:333
  173.8 4.5 %copy.18 = f32[4,128,2240]{1,2,0:T(8,128)} copy(bf16[4,128,2240]{2,1,0:T(8,128)(2,1)} %bitcast.45) | data formatting | bytes 6881280 | tf_op jit(solution)/shard_map/convert_element_type | solution.py:337
  178.3 4.5 %copy.19 = f32[4,128,2240]{1,2,0:T(8,128)} copy(bf16[4,128,2240]{2,1,0:T(8,128)(2,1)} %bitcast.44) | data formatting | bytes 6881280 | tf_op jit(solution)/shard_map/convert_element_type | solution.py:337
  182.8 3.0 %copy.20 = f32[4,128,2240]{1,2,0:T(8,128)} copy(bf16[4,128,2240]{2,1,0:T(8,128)(2,1)S(1)} %bitcast.43) | data formatting | bytes 6881280 | tf_op jit(solution)/shard_map/convert_element_type | solution.py:337
  185.9 0.1 slice_reduce_fusion.2
  185.9 7.2 %add_convert_fusion = bf16[4,128,2240]{1,2,0:T(8,128)(2,1)} fusion(f32[4,128,2240]{1,2,0:T(8,128)} %copy.20, f32[4,128,2240]{1,2,0:T(8,128)} %copy.19, f32[4,128,2240]{1,2,0:T(8,128)} %copy.18, f32[2240]{0:T(1024)S(1)} %get-tuple-element.12, f32[2240]{0:T(1024)S(1)} %get-tuple-element.13, f32[2240]{0:T(1024)S(1)} %get-tuple-element.11), kind=kLoop, calls=%fused_computation.4 | loop fusion | flops 6881280 | bytes 16083200 | tf_op jit(solution)/shard_map/convert_element_type | solution.py:338
  (9 shorter events, 0.0 us)
Async XLA Ops:
  6.3 1.8 copy-start.5
  12.3 1.6 copy-start
  13.9 1.3 copy-start.1
  125.3 2.8 %copy-start.2 = (bf16[4,128,2240]{1,2,0:T(8,128)(2,1)S(1)}, bf16[4,128,2240]{1,2,0:T(8,128)(2,1)}, u32[]{:S(2)}) copy-start(bf16[4,128,2240]{1,2,0:T(8,128)(2,1)} %param.5) | copy-start | bytes 6881284
  146.2 8.9 %copy-start.4 = (bf16[768,8,288]{0,2,1:T(8,128)(2,1)S(1)}, bf16[768,8,288]{0,2,1:T(8,128)(2,1)}, u32[]{:S(2)}) copy-start(bf16[768,8,288]{0,2,1:T(8,128)(2,1)} %pad.15) | copy-start | bytes 10616836
  155.1 7.5 %copy-start.3 = (bf16[1,8,288,1152]{3,2,1,0:T(8,128)(2,1)S(1)}, bf16[1,8,288,1152]{3,2,1,0:T(8,128)(2,1)}, u32[]{:S(2)}) copy-start(bf16[1,8,288,1152]{3,2,1,0:T(8,128)(2,1)} %get-tuple-element.14) | copy-start | bytes 15925252
  182.8 3.1 %copy-start.6 = (f32[3,2240]{1,0:T(4,128)S(1)}, f32[3,2240]{1,0:T(4,128)}, u32[]{:S(2)}) copy-start(f32[3,2240]{1,0:T(4,128)} %param.9) | copy-start | bytes 80644

commit v2 on v1

--- a/solution.py
+++ b/solution.py
@@ -295,6 +295,115 @@
     )(kv, weight, queries)
 
 
+def cuts(start, stop, size):
+    while start < stop:
+        end = min(stop, (start // size + 1) * size)
+        yield start, end
+        start = end
+
+
+def project(deep, q_ref, early_ref, states_ref, w_hbm, taps_ref, out_ref, w_ref, att_ref, w_sem):
+    frames, tokens, width = q_ref.shape
+    lanes_y, rows = states_ref.shape[1], states_ref.shape[3]
+    deep_pad, half = w_hbm.shape[2], w_hbm.shape[3]
+    sections = w_hbm.shape[1]
+    loads = [pltpu.make_async_copy(w_hbm.at[n], w_ref.at[n], w_sem.at[n]) for n in range(2)]
+    for load in loads:
+        load.start()
+
+    def attend(f, query):
+        span = pl.ds(pl.multiple_of(f * tokens, 16), tokens)
+        for h in range(HEADS):
+            low, high = h * HEAD_DIM, (h + 1) * HEAD_DIM
+            state = [states_ref[(p // rows) // lanes_y, (p // rows) % lanes_y, f, p % rows:p % rows + e - p]
+                     for p, e in cuts(low, high, rows)]
+            state = state[0] if len(state) == 1 else jnp.concatenate(state, axis=0)
+            sums = jnp.dot(query(low, high), state, preferred_element_type=jnp.float32)
+            scale = 1.0 / (sums[:, HEAD_DIM:HEAD_DIM + 1] + stab_eps)
+            result = (sums * scale).astype(jnp.bfloat16)
+            for p, e in cuts(low, high, deep):
+                to = p // deep * deep_pad + p % deep
+                att_ref[span, to:to + e - p] = result[:, p - low:e - low]
+
+    for n in range(sections):
+        att_ref[:, n * deep_pad + deep:(n + 1) * deep_pad] = jnp.zeros(
+            (att_ref.shape[0], deep_pad - deep), jnp.bfloat16)
+
+    first = lax.axis_index("frame") == 0
+
+    @pl.when(first)
+    def _():
+        att_ref[0:HALO * tokens] = jnp.zeros((HALO * tokens, att_ref.shape[1]), jnp.bfloat16)
+
+    @pl.when(jnp.logical_not(first))
+    def _():
+        @pl.loop(0, HALO)
+        def _(f):
+            attend(f, lambda low, high: jnp.maximum(early_ref[f, :, low:high], 0))
+
+    @pl.loop(0, frames)
+    def _(f):
+        attend(f + HALO, lambda low, high: jnp.maximum(q_ref[f, :, low:high], 0))
+
+    def columns(weight, start, count):
+        result = jnp.dot(att_ref[...], weight, preferred_element_type=jnp.float32)
+        result = result.astype(jnp.bfloat16).astype(jnp.float32)
+        result = result.reshape(HALO + frames, tokens, weight.shape[1])[:, :, :count]
+        span = pl.ds(start, count)
+        mixed = (taps_ref[0:1, span] * result[HALO:] + taps_ref[1:2, span] * result[1:-1]
+                 + taps_ref[2:3, span] * result[:-HALO])
+        out_ref[:, :, span] = mixed.astype(jnp.bfloat16)
+
+    deepest = sections * deep_pad
+    step = 2 * LANES
+    whole = half // step
+    rest = half - whole * step
+
+    def weight(n, span):
+        return w_ref[n, :, :, span].reshape(deepest, span.size)
+
+    loads[0].wait()
+
+    @pl.loop(0, whole)
+    def _(t):
+        at = pl.multiple_of(t * step, step)
+        columns(weight(0, pl.ds(at, step)), at, step)
+
+    loads[1].wait()
+    if rest:
+        both = jnp.concatenate([weight(0, pl.ds(half - rest, rest)), weight(1, pl.ds(0, rest))], axis=1)
+        columns(both, half - rest, 2 * rest)
+
+    @pl.loop(0, whole - 1)
+    def _(t):
+        at = pl.multiple_of(t * step + rest, LANES)
+        columns(weight(1, pl.ds(at, step)), pl.multiple_of(half + at, step), step)
+
+    at = (whole - 1) * step + rest
+    columns(weight(1, pl.ds(at, step)), half + at, width - half - at)
+
+
+def projection(queries, earlier, states, weight, taps, deep):
+    frames, tokens, width = queries.shape
+    rows = (HALO + frames) * tokens
+    depth = weight.shape[1] * weight.shape[2]
+    whole = pl.BlockSpec(memory_space=pltpu.VMEM)
+    return pl.pallas_call(
+        functools.partial(project, deep),
+        out_shape=jax.ShapeDtypeStruct(queries.shape, queries.dtype),
+        in_specs=[whole, whole, whole, pl.BlockSpec(memory_space=pl.ANY), whole],
+        out_specs=whole,
+        scratch_shapes=[
+            pltpu.VMEM(weight.shape, weight.dtype),
+            pltpu.VMEM((rows, depth), jnp.bfloat16),
+            pltpu.SemaphoreType.DMA((2,)),
+        ],
+        cost_estimate=pl.CostEstimate(
+            flops=2 * rows * depth * width, bytes_accessed=2 * depth * width, transcendentals=0),
+        compiler_params=pltpu.CompilerParams(vmem_limit_bytes=50 * 2**20),
+    )(queries, earlier, states, weight, taps)
+
+
 def up_to(value, multiple):
     return -(-value // multiple) * multiple
 
@@ -318,24 +427,7 @@
     weight = jnp.pad(out_weight, ((0, deep_pad - deep), (0, wide - width)))
     weight = weight.reshape(deep_pad, 2, wide // 2).transpose(1, 0, 2)
     states, weight, earlier = exchanged(kv, weight, queries, outer, lanes_y)
-    states = states.transpose(2, 0, 1, 3, 4).reshape(HALO + frames, tall, LANES)[:, :width]
-    states = states.reshape(HALO + frames, HEADS, HEAD_DIM, LANES)
-    first = lax.axis_index("frame") == 0
-    earlier = jnp.where(first, jnp.zeros_like(earlier), earlier)
-    query_relu = jax.nn.relu(jnp.concatenate([earlier, queries], axis=0))
-    query_relu = query_relu.reshape(HALO + frames, tokens, HEADS, HEAD_DIM)
-    sums = jnp.einsum("fshd,fhde->fshe", query_relu, states, preferred_element_type=jnp.float32)
-    attention = sums[..., :HEAD_DIM] / (sums[..., HEAD_DIM:HEAD_DIM + 1] + stab_eps)
-    attention = attention.astype(jnp.bfloat16).reshape((HALO + frames) * tokens, sections, deep)
-    attention = jnp.pad(attention, ((0, 0), (0, 0), (0, deep_pad - deep)))
-    attention = attention.reshape((HALO + frames) * tokens, sections * deep_pad)
-    weight = weight.reshape(2, sections * deep_pad, wide // 2)
-    projected = jnp.concatenate(
-        [jnp.dot(attention, weight[n], preferred_element_type=jnp.float32).astype(jnp.bfloat16)
-         for n in range(2)], axis=1)[:, :width]
-    extended = projected.reshape(HALO + frames, tokens, width)
-    mixed = conv_taps[0] * extended[2:] + conv_taps[1] * extended[1:-1] + conv_taps[2] * extended[:-2]
-    return mixed.astype(jnp.bfloat16)
+    return projection(queries, earlier, states, weight, conv_taps, deep)
 
 
 def solution(mesh):

time: 194 us -> 162 us (0.84)
  local copies, waits for them, and re-layouts: 50.5 us -> 15.9 us
  Pallas kernels: 108 us -> 140 us
  other arithmetic: 17.5 us -> 1.53 us
  matrix products: 17 us -> 3.78 us
    pallas_call x0 -> x1, Pallas kernels: none -> 32.3 us  [projection(): pl.pallas_call(functools.partial(project, deep), out_shape=jax.ShapeDtype...]
    convert_element_type x4 -> x0, local copies, waits for them, and re-layouts: 16.6 us -> none  [the longest x1 4.55 us: per_device(): conv_taps[1] * extended[1:-1]]
    dot_general x3 -> x0, matrix products: 15.6 us -> none  [the longest x2 12.3 us: per_device(): jnp.dot(attention, weight[n], preferred_element_type=jnp.float32)]
    slice x2 -> x0, local copies, waits for them, and re-layouts: 8.98 us -> none  [the longest x1 8.9 us: per_device(): weight[n]]
    convert_element_type x2 -> x0, other arithmetic: 8.19 us -> none  [the longest x1 7.18 us: per_device(): return mixed.astype(jnp.bfloat16)]
    reshape x1 -> x0, local copies, waits for them, and re-layouts: 7.01 us -> none  [per_device(): attention.astype(jnp.bfloat16)]
    concatenate x1 -> x0, other arithmetic: 6.4 us -> none  [per_device(): jnp.concatenate([jnp.dot(attention, weight[n], preferred_element_type=jnp...]
    dot_general x1, matrix products: 1.35 us -> 3.78 us  [per_device(): jnp.einsum('fshd,fshe->fhde', key_relu, rows, preferred_element_type=jnp....]
where the time goes in v2:
time: 162 us; the launch traced here: 161 us
  Pallas kernels  140 us (86%)
  local copies, waits for them, and re-layouts  15.9 us (10%)
  matrix products  3.78 us (2%)
    pallas_call x1, Pallas kernels, exchanged(): pl.pallas_call(functools.partial(exchange, outer, lanes_y), out_shape=(ja...  108 us
    pallas_call x1, Pallas kernels, projection(): pl.pallas_call(functools.partial(project, deep), out_shape=jax.ShapeDtype...  32.3 us
    unnamed x11, local copies, waits for them, and re-layouts  5.81 us
    reshape x1, local copies, waits for them, and re-layouts, per_device(): rows = values.reshape(frames, tokens, HEADS, HEAD_DIM)  4.75 us
    dot_general x1, matrix products, per_device(): jnp.einsum('fshd,fshe->fhde', key_relu, rows, preferred_element_type=jnp....  3.78 us

profile of v2, /device:TPU:31, one launch (start us, length us, event | category | flops | bytes accessed | tf_op | source)
XLA Modules:
  0.0 161.4 jit_solution(13474819139402863417)
XLA Ops:
  0.0 0.0 copy-start.4
  0.0 1.6 pad.10
  1.6 1.2 copy.19
  2.7 0.0 copy-done.4
  2.7 1.5 broadcast_maximum_fusion
  4.3 2.8 %copy.13.q_in.q_ref = bf16[4,128,2240]{2,1,0:T(8,128)(2,1)S(1)} copy(bf16[4,128,2240]{1,2,0:T(8,128)(2,1)} %param.5) | data formatting | bytes 4587520 | tf_op args[0]
  7.1 0.0 copy-start
  7.1 4.8 %copy.9 = bf16[4,128,20,112]{3,1,2,0:T(8,128)(2,1)} copy(bf16[4,128,20,112]{1,3,2,0:T(8,128)(2,1)} %bitcast.17) | data formatting | bytes 4587520 | tf_op jit(solution)/shard_map/reshape | solution.py:416
  11.9 3.8 %fusion.5 = bf16[4,20,112,128]{3,2,1,0:T(8,128)(2,1)S(1)} fusion(bf16[4,128,20,112]{1,3,2,0:T(8,128)(2,1)} %bitcast.18, bf16[4,128,20,112]{3,1,2,0:T(8,128)(2,1)} %copy.9), kind=kOutput, calls=%fused_computation.6 | convolution fusion | flops 297369600 | bytes 6881280 | tf_op jit(solution)/shard_map/fshd,fshe->fhde/dot_general | solution.py:419
  15.6 0.0 copy-start.1
  15.6 0.2 copy.18
  15.8 0.0 copy-done
  15.8 1.1 copy-done.1
  17.0 0.0 copy-start.3
  17.0 107.9 %shard_map.55 = (bf16[2,2,6,560,128]{4,3,2,1,0:T(8,128)(2,1)S(1)}, bf16[2,8,288,1152]{3,2,1,0:T(8,128)(2,1)}, bf16[2,128,2240]{2,1,0:T(8,128)(2,1)S(1)}) custom-call(bf16[2,2,4,560,128]{4,3,2,1,0:T(8,128)(2,1)S(1)} %bitcast.14, bf16[2,288,1152]{2,1,0:T(8,128)(2,1)S(1)} %bitcast.15, bf16[4,128,2240]{2,1,0:T(8,128)(2,1)S(1)} %copy.13.q_in.q_ref), custom_call_target="tpu_custom_call" | custom-call | tf_op jit(solution)/shard_map/pallas_call | solution.py:264
  124.9 0.0 copy-start.2
  124.9 1.8 %copy-done.2 = bf16[2,2,6,560,128]{4,3,2,1,0:T(8,128)(2,1)} copy-done((bf16[2,2,6,560,128]{4,3,2,1,0:T(8,128)(2,1)}, bf16[2,2,6,560,128]{4,3,2,1,0:T(8,128)(2,1)S(1)}, u32[]{:S(2)}) %copy-start.2) | copy-done | bytes 3440664
  126.7 0.0 copy-done.3
  126.7 32.3 %shard_map.56 = bf16[4,128,2240]{2,1,0:T(8,128)(2,1)S(1)} custom-call(bf16[4,128,2240]{2,1,0:T(8,128)(2,1)} %copy-done, bf16[2,128,2240]{2,1,0:T(8,128)(2,1)S(1)} %get-tuple-element.8.early_ref, bf16[2,2,6,560,128]{4,3,2,1,0:T(8,128)(2,1)} %copy-done.2, bf16[2,8,288,1152]{3,2,1,0:T(8,128)(2,1)} %get-tuple-element.10.w_hbm, f32[3,2240]{1,0:T(4,128)S(1)} %copy-done.3), custom_call_target="tpu_custom_call" | custom-call | flops 7927234560 | bytes 10321920 | tf_op jit(solution)/shard_map/pallas_call | solution.py:391
  159.0 2.4 %copy.14 = bf16[4,128,2240]{1,2,0:T(8,128)(2,1)} copy(bf16[4,128,2240]{2,1,0:T(8,128)(2,1)S(1)} %shard_map.56) | data formatting | bytes 4587520 | tf_op jit(solution)/shard_map/pallas_call | solution.py:391
Async XLA Ops:
  0.0 2.7 %copy-start.4 = (bf16[4,128,2240]{1,2,0:T(8,128)(2,1)S(1)}, bf16[4,128,2240]{1,2,0:T(8,128)(2,1)}, u32[]{:S(2)}) copy-start(bf16[4,128,2240]{1,2,0:T(8,128)(2,1)} %param.6) | copy-start | bytes 6881284
  7.1 8.7 %copy-start = (bf16[4,128,2240]{2,1,0:T(8,128)(2,1)}, bf16[4,128,2240]{2,1,0:T(8,128)(2,1)S(1)}, u32[]{:S(2)}) copy-start(bf16[4,128,2240]{2,1,0:T(8,128)(2,1)S(1)} %copy.13.q_in.q_ref) | copy-start | bytes 6881284
  15.6 1.3 copy-start.1
  17.0 109.8 %copy-start.3 = (f32[3,2240]{1,0:T(4,128)S(1)}, f32[3,2240]{1,0:T(4,128)}, u32[]{:S(2)}) copy-start(f32[3,2240]{1,0:T(4,128)} %taps_ref.1) | copy-start | bytes 80644
  124.9 1.8 %copy-start.2 = (bf16[2,2,6,560,128]{4,3,2,1,0:T(8,128)(2,1)}, bf16[2,2,6,560,128]{4,3,2,1,0:T(8,128)(2,1)S(1)}, u32[]{:S(2)}) copy-start(bf16[2,2,6,560,128]{4,3,2,1,0:T(8,128)(2,1)S(1)} %get-tuple-element.9.states_ref) | copy-start | bytes 10321924

commit v3 on v2

v3 whole, which is shorter than its diff:
```python
import functools

import jax
import jax.numpy as jnp
from jax import lax
from jax.experimental import pallas as pl
from jax.experimental.pallas import tpu as pltpu
from jax.sharding import PartitionSpec as P

HEADS = 20
HEAD_DIM = 112
LANES = 128
HALO = 2
stab_eps = 1e-06
MESH = pl.DeviceIdType.MESH


def cuts(start, stop, size):
    while start < stop:
        end = min(stop, (start // size + 1) * size)
        yield start, end
        start = end


def exchange(outer, lanes_y, k_in, v_in, w_in, q_in, cum_out, pre_out, w_out, q_out,
             kv_in, sib_kv, chip_kv, y_kv, frame_kv, cum, pre, x_got, pair_msg, edge_msg, pair_got, edge_got,
             own_sem, kv_sem, z_sem, x_sem, y_sem, sz_sem, sx_sem, sy_sem, p_sem):
    frame = lax.axis_index("frame")
    space = lax.axis_index("space")
    o, i = frame // 2, frame % 2
    y, c = space // 2, space % 2
    frames, tall = kv_in.shape[2], kv_in.shape[3]
    rows = w_in.shape[1]
    part = rows // lanes_y

    def at(o_=None, i_=None, y_=None, c_=None):
        o_ = o if o_ is None else o_
        i_ = i if i_ is None else i_
        y_ = y if y_ is None else y_
        c_ = c if c_ is None else c_
        return (o_ * 2 + i_, y_ * 2 + c_)

    def copy(src, dst, sems, to):
        return pltpu.make_async_remote_copy(
            src_ref=src, dst_ref=dst, send_sem=sems.at[0], recv_sem=sems.at[1],
            device_id=to, device_id_type=MESH)

    def when(cond, do):
        if cond is True:
            do()
        else:
            pl.when(cond)(do)

    def y_far(d):
        return lax.rem(y + d, lanes_y)

    def y_from(d):
        return lax.rem(y + lanes_y - d, lanes_y)

    barrier = pltpu.get_barrier_semaphore()

    def greet(to):
        pl.semaphore_signal(barrier, inc=1, device_id=to, device_id_type=MESH)

    for d in range(1, outer):
        greet(at(o_=lax.rem(o + d, outer)))
    for d in range(1, lanes_y):
        greet(at(y_=y_far(d)))
    greet(at(i_=1 - i))
    greet(at(c_=1 - c))
    into = jnp.logical_and(i == 0, o > 0)
    onto = jnp.logical_and(i == 1, o < outer - 1)
    when(into, lambda: greet(at(o_=o - 1, i_=1)))
    when(onto, lambda: greet(at(o_=o + 1, i_=0)))
    peers = (outer - 1) + (lanes_y - 1) + 2
    pl.semaphore_wait(barrier, peers + jnp.where(jnp.logical_or(into, onto), 1, 0))

    def source(key):
        t = (key + 1) // 2
        if key == 0:
            return o, True
        if key % 2:
            return o - t, o >= t
        return o + t, o + t < outer

    keys = range(2 * outer - 1)
    sent = []

    def launch(cond, make):
        when(cond, lambda: make().start())
        sent.append((cond, make))

    def mine(key):
        return w_out.at[c, source(key)[0] * 2 + i]

    def theirs(key, y_):
        span = pl.ds(pl.multiple_of(y_ * part, 16), part)
        return w_out.at[c, source(key)[0] * 2 + 1 - i, span]

    def z_copy(up, t):
        g = ((o - t + 1) if up else (o + t - 1)) * 2 + i
        dst = w_out.at[c, g]
        return copy(w_in.at[c] if t == 1 else dst, dst, z_sem.at[0 if up else 1, t],
                    at(o_=o + 1 if up else o - 1))

    def z_send(t):
        launch(jnp.logical_and(o < outer - 1, o - t + 1 >= 0), lambda: z_copy(True, t))
        launch(jnp.logical_and(o > 0, o + t - 1 < outer), lambda: z_copy(False, t))

    def z_wait(t):
        def got(key, up):
            ref = mine(key)
            copy(ref, ref, z_sem.at[0 if up else 1, t], at(c_=1 - c)).wait_recv()
        when(source(2 * t - 1)[1], lambda: got(2 * t - 1, True))
        when(source(2 * t)[1], lambda: got(2 * t, False))

    def x_copy(key):
        span = pl.ds(pl.multiple_of(y * part, 16), part)
        src = w_in.at[c, span] if key == 0 else mine(key).at[span]
        return copy(src, mine(key).at[span], x_sem.at[key], at(i_=1 - i))

    def x_send(key):
        launch(source(key)[1], lambda: x_copy(key))

    def sib_z(key):
        launch(source(key)[1], lambda: copy(mine(key), mine(key), sz_sem.at[key], at(c_=1 - c)))

    def x_pass(key):
        def got():
            ref = theirs(key, y)
            copy(ref, ref, x_sem.at[key], at(i_=1 - i)).wait_recv()
        cond = source(key)[1]
        when(cond, got)
        for d in range(1, lanes_y):
            launch(cond, lambda d=d: copy(theirs(key, y), theirs(key, y), y_sem.at[key, d],
                                          at(y_=y_far(d))))
        launch(cond, lambda: copy(theirs(key, y), theirs(key, y), sx_sem.at[key], at(c_=1 - c)))

    def y_pass(key):
        cond = source(key)[1]
        for d in range(1, lanes_y):
            def got(d=d):
                ref = theirs(key, y_from(d))
                copy(ref, ref, y_sem.at[key, d], at(y_=y_far(d))).wait_recv()
            when(cond, got)
            launch(cond, lambda d=d: copy(theirs(key, y_from(d)), theirs(key, y_from(d)),
                                          sy_sem.at[key, d], at(c_=1 - c)))

    def sib_wait(key):
        cond = source(key)[1]
        g = source(key)[0] * 2

        def got(ref, sems):
            copy(ref, ref, sems, at(c_=1 - c)).wait_recv()
        if key:
            when(cond, lambda: got(w_out.at[1 - c, g + i], sz_sem.at[key]))
        for d in range(lanes_y):
            span = pl.ds(pl.multiple_of(y_from(d) * part, 16), part)
            sems = sx_sem.at[key] if d == 0 else sy_sem.at[key, d]
            when(cond, lambda span=span, sems=sems: got(w_out.at[1 - c, g + 1 - i, span], sems))

    z_send(1)
    x_send(0)
    locals_ = [pltpu.make_async_copy(w_in, w_out.at[:, frame], own_sem.at[0])]
    locals_[0].start()

    def halo(f):
        launch(frame < 2 * outer - 1,
               lambda: copy(q_in.at[frames - HALO + f], q_out.at[f], p_sem.at[f], (frame + 1, space)))

    tokens = k_in.shape[2]
    gap = LANES - HEAD_DIM
    nothing = jnp.zeros((gap, tokens), jnp.bfloat16)
    ones = jnp.ones((gap, tokens), jnp.bfloat16)

    @pl.loop(0, frames)
    def _(f):
        for h in range(HEADS):
            span = slice(h * HEAD_DIM, (h + 1) * HEAD_DIM)
            key = jnp.concatenate([jnp.maximum(k_in[f, span], 0), nothing], axis=0)
            value = jnp.concatenate([v_in[f, span], ones], axis=0)
            sums = lax.dot_general(value, key, (((1,), (1,)), ((), ())),
                                   preferred_element_type=jnp.float32).astype(jnp.bfloat16)
            for p, e in cuts(h * LANES, (h + 1) * LANES, tall):
                n = p // tall
                kv_in[n // lanes_y, n % lanes_y, f, p % tall:p % tall + e - p] = (
                    sums[p - h * LANES:e - h * LANES])

    sib_copy = copy(kv_in.at[1 - c], sib_kv, kv_sem.at[0], at(c_=1 - c))
    sib_copy.start()
    sib_copy.wait_recv()
    for d in list(range(1, lanes_y)) + [0]:
        to = y_far(d)
        for f in range(frames):
            chip_kv[to, f] = (kv_in[c, to, f].astype(jnp.float32)
                              + sib_kv[to, f].astype(jnp.float32)).astype(jnp.bfloat16)
        if d:
            launch(True, lambda d=d: copy(chip_kv.at[y_far(d)], y_kv.at[d], kv_sem.at[3 + d],
                                          at(y_=y_far(d))))
    halo(0)
    z_wait(1)
    if outer > 2:
        z_send(2)
    for key in (1, 2):
        x_send(key)
        sib_z(key)
    for d in range(1, lanes_y):
        copy(chip_kv.at[y_far(d)], y_kv.at[d], kv_sem.at[3 + d], at(y_=y_far(d))).wait_recv()
    for f in range(frames):
        total = chip_kv[y, f].astype(jnp.float32)
        for d in range(1, lanes_y):
            total = total + y_kv[d, f].astype(jnp.float32)
        frame_kv[f] = total if f == 0 else frame_kv[f - 1] + total
    for f in range(HALO):
        x_got[0, f] = frame_kv[frames - 1 - f].astype(jnp.bfloat16)
    launch(True, lambda: copy(x_got.at[0], x_got.at[1], p_sem.at[HALO], at(i_=1 - i)))
    for f in range(frames):
        cum[f] = frame_kv[f].astype(jnp.bfloat16)
    for d in range(1, lanes_y):
        launch(True, lambda d=d: copy(cum, cum_out.at[c, y], kv_sem.at[3 + lanes_y + d], at(y_=y_far(d))))
    locals_.append(pltpu.make_async_copy(cum, cum_out.at[c, y], own_sem.at[1]))
    locals_[1].start()
    x_pass(0)

    def pair():
        copy(x_got.at[0], x_got.at[1], p_sem.at[HALO], at(i_=1 - i)).wait_recv()
        pair_msg[...] = (x_got[0, 0].astype(jnp.float32) + x_got[1, 0].astype(jnp.float32)).astype(jnp.bfloat16)
        low = jnp.where(i == 0, x_got[0, 0].astype(jnp.float32), x_got[1, 0].astype(jnp.float32))
        high = jnp.where(i == 0, x_got[1, 1].astype(jnp.float32), x_got[0, 1].astype(jnp.float32))
        edge_msg[...] = (low + high).astype(jnp.bfloat16)
        for d in range(1, outer):
            launch(o + d < outer,
                   lambda d=d: copy(pair_msg, pair_got.at[d], p_sem.at[HALO + 1 + d], at(o_=o + d)))
        launch(o + 1 < outer, lambda: copy(edge_msg, edge_got, p_sem.at[HALO + 1], at(o_=o + 1)))

    def prefix():
        for d in range(1, outer):
            when(o >= d, lambda d=d: copy(pair_msg, pair_got.at[d], p_sem.at[HALO + 1 + d],
                                          at(c_=1 - c)).wait_recv())
        when(o >= 1, lambda: copy(edge_msg, edge_got, p_sem.at[HALO + 1], at(c_=1 - c)).wait_recv())
        zero = jnp.zeros(pair_msg.shape, jnp.float32)
        far = zero
        for d in range(2, outer):
            far = far + jnp.where(o >= d, pair_got[d].astype(jnp.float32), zero)
        near = jnp.where(o >= 1, pair_got[1].astype(jnp.float32), zero)
        edge = jnp.where(o >= 1, edge_got[...].astype(jnp.float32), zero)
        base = far + near
        before = jnp.where(i == 0, base, base + x_got[1, 0].astype(jnp.float32))
        second = jnp.where(i == 0, far + edge, base + x_got[1, 1].astype(jnp.float32))
        pre[0] = second.astype(jnp.bfloat16)
        pre[1] = before.astype(jnp.bfloat16)
        for d in range(1, lanes_y):
            launch(True, lambda d=d: copy(pre, pre_out.at[c, y], kv_sem.at[3 + 2 * lanes_y + d],
                                          at(y_=y_far(d))))
        locals_.append(pltpu.make_async_copy(pre, pre_out.at[c, y], own_sem.at[2]))
        locals_[2].start()

    def hand_on(out, first, own, sems):
        for d in range(1, lanes_y):
            ref = out.at[c, y_from(d)]
            copy(ref, ref, kv_sem.at[first + d], at(y_=y_far(d))).wait_recv()
        own.wait()
        launch(True, lambda: copy(out.at[c], out.at[c], sems, at(c_=1 - c)))

    for t in range(2, outer):
        z_wait(t)
        if t + 1 < outer:
            z_send(t + 1)
        for key in (2 * t - 1, 2 * t):
            x_send(key)
            sib_z(key)
        if t == 2:
            pair()
            halo(1)
        for key in (2 * t - 3, 2 * t - 2):
            x_pass(key)
        for key in ((0,) if t == 2 else (2 * t - 5, 2 * t - 4)):
            y_pass(key)
    if outer <= 2:
        pair()
        halo(1)
        y_pass(0)
    prefix()
    if outer > 2:
        for key in (2 * outer - 5, 2 * outer - 4):
            y_pass(key)
    hand_on(cum_out, 3 + lanes_y, locals_[1], kv_sem.at[1])
    for key in (2 * outer - 3, 2 * outer - 2):
        x_pass(key)
    hand_on(pre_out, 3 + 2 * lanes_y, locals_[2], kv_sem.at[2])
    for key in (2 * outer - 3, 2 * outer - 2):
        y_pass(key)

    for out, sems in ((cum_out, kv_sem.at[1]), (pre_out, kv_sem.at[2])):
        other = out.at[1 - c]
        copy(other, other, sems, at(c_=1 - c)).wait_recv()
    for f in range(HALO):
        ref = q_out.at[f]
        when(frame > 0, lambda f=f, ref=ref: copy(ref, ref, p_sem.at[f], at(c_=1 - c)).wait_recv())
    for key in keys:
        sib_wait(key)
    locals_[0].wait()
    sib_copy.wait_send()
    for cond, make in sent:
        when(cond, lambda make=make: make().wait_send())


def exchanged(keys, values, weight, queries, tall, outer, lanes_y):
    frames = keys.shape[0]
    count = 2 * outer - 1
    tile = (tall, LANES)
    half = jnp.bfloat16
    dma = pltpu.SemaphoreType.DMA
    whole = pl.BlockSpec(memory_space=pltpu.VMEM)
    anywhere = pl.BlockSpec(memory_space=pl.ANY)
    return pl.pallas_call(
        functools.partial(exchange, outer, lanes_y),
        out_shape=(
            jax.ShapeDtypeStruct((2, lanes_y, frames) + tile, half),
            jax.ShapeDtypeStruct((2, lanes_y, HALO) + tile, half),
            jax.ShapeDtypeStruct((2, 2 * outer) + weight.shape[1:], half),
            jax.ShapeDtypeStruct((HALO,) + queries.shape[1:], half),
        ),
        in_specs=[whole, whole, anywhere, anywhere],
        out_specs=(anywhere,) * 4,
        scratch_shapes=[
            pltpu.VMEM((2, lanes_y, frames) + tile, half),
            pltpu.VMEM((lanes_y, frames) + tile, half),
            pltpu.VMEM((lanes_y, frames) + tile, half),
            pltpu.VMEM((lanes_y, frames) + tile, half),
            pltpu.VMEM((frames,) + tile, jnp.float32),
            pltpu.VMEM((frames,) + tile, half),
            pltpu.VMEM((HALO,) + tile, half),
            pltpu.VMEM((2, HALO) + tile, half),
            pltpu.VMEM(tile, half),
            pltpu.VMEM(tile, half),
            pltpu.VMEM((outer,) + tile, half),
            pltpu.VMEM(tile, half),
            dma((3,)),
            dma((3 + 3 * lanes_y, 2)),
            dma((2, outer, 2)),
            dma((count, 2)),
            dma((count, lanes_y, 2)),
            dma((count, 2)),
            dma((count, 2)),
            dma((count, lanes_y, 2)),
            dma((HALO + 1 + outer, 2)),
        ],
        compiler_params=pltpu.CompilerParams(
            collective_id=0, has_side_effects=True, vmem_limit_bytes=40 * 2**20),
    )(keys, values, weight, queries)


def project(deep, q_hbm, early_hbm, cum_hbm, pre_hbm, w_hbm, taps_ref, out_ref,
            q_ref, early_ref, cum_ref, pre_ref, w_ref, head_ref, att_ref, sems):
    frames, width, tokens = q_ref.shape
    lanes_y, rows = cum_ref.shape[1], cum_ref.shape[3]
    sections, deep_pad, half = w_hbm.shape[1:]
    moves = [(q_hbm, q_ref), (early_hbm, early_ref), (pre_hbm, pre_ref), (cum_hbm, cum_ref),
             (w_hbm.at[0], w_ref.at[0]), (w_hbm.at[1], w_ref.at[1])]
    loads = [pltpu.make_async_copy(src, dst, sems.at[n]) for n, (src, dst) in enumerate(moves)]
    for load in loads:
        load.start()
    gap = jnp.zeros((LANES - HEAD_DIM, tokens), jnp.bfloat16)
    head_ref[...] = jnp.zeros(head_ref.shape, jnp.bfloat16)

    def place(channel):
        section, at = channel // deep, channel % deep
        return section * deep_pad + section * deep % 16 + at

    def state(ref, f, h):
        pieces = [ref[(p // rows) // lanes_y, (p // rows) % lanes_y, f, p % rows:p % rows + e - p]
                  for p, e in cuts(h * LANES, (h + 1) * LANES, rows)]
        return pieces[0] if len(pieces) == 1 else jnp.concatenate(pieces, axis=0)

    def attend(f, query, states):
        for h in range(HEADS):
            low, high = h * HEAD_DIM, (h + 1) * HEAD_DIM
            rows_in = jnp.maximum(query(low, high), 0)
            terms = states(h)
            sums = jnp.dot(jnp.concatenate(terms, axis=1),
                           jnp.concatenate([rows_in, gap] * len(terms), axis=0),
                           preferred_element_type=jnp.float32)
            result = sums[:HEAD_DIM] * (1.0 / (sums[HEAD_DIM:HEAD_DIM + 1] + stab_eps))
            pieces, end = [], None
            for p, e in cuts(low, high, deep):
                if end is not None:
                    pieces.append(jnp.zeros((place(p) - end, tokens), jnp.float32))
                pieces.append(result[p - low:e - low])
                end = place(e - 1) + 1
            result = pieces[0] if len(pieces) == 1 else jnp.concatenate(pieces, axis=0)
            head_ref[place(low):end] = result.astype(jnp.bfloat16)
        span = pl.ds(pl.multiple_of(f * tokens, LANES), tokens)
        att_ref[span] = head_ref[...].T

    first = lax.axis_index("frame") == 0
    for load in loads[:3]:
        load.wait()

    @pl.when(first)
    def _():
        att_ref[0:HALO * tokens] = jnp.zeros((HALO * tokens, att_ref.shape[1]), jnp.bfloat16)

    @pl.when(jnp.logical_not(first))
    def _():
        @pl.loop(0, HALO)
        def _(f):
            attend(f, lambda low, high: early_ref[f, low:high], lambda h: [state(pre_ref, f, h)])

    loads[3].wait()

    @pl.loop(0, frames)
    def _(f):
        attend(f + HALO, lambda low, high: q_ref[f, low:high],
               lambda h: [state(pre_ref, 1, h), state(cum_ref, f, h)])

    def columns(weight, start, count):
        result = jnp.dot(att_ref[...], weight, preferred_element_type=jnp.float32)
        result = result.astype(jnp.bfloat16).astype(jnp.float32)
        result = result.reshape(HALO + frames, tokens, weight.shape[1])[:, :, :count]
        span = pl.ds(start, count)
        taps = [taps_ref[n:n + 1, span] for n in range(3)]
        for f in range(frames):
            mixed = taps[0] * result[f + 2] + taps[1] * result[f + 1] + taps[2] * result[f]
            out_ref[f, span] = mixed.T.astype(jnp.bfloat16)

    deepest = sections * deep_pad
    step = 2 * LANES
    whole = half // step
    rest = half - whole * step

    def weight(n, span):
        return w_ref[n, :, :, span].reshape(deepest, span.size)

    loads[4].wait()

    @pl.loop(0, whole)
    def _(t):
        at = pl.multiple_of(t * step, step)
        columns(weight(0, pl.ds(at, step)), at, step)

    loads[5].wait()
    if rest:
        both = jnp.concatenate([weight(0, pl.ds(half - rest, rest)), weight(1, pl.ds(0, rest))], axis=1)
        columns(both, half - rest, 2 * rest)

    @pl.loop(0, whole - 1)
    def _(t):
        at = pl.multiple_of(t * step + rest, LANES)
        columns(weight(1, pl.ds(at, step)), pl.multiple_of(half + at, LANES), step)

    at = (whole - 1) * step + rest
    columns(weight(1, pl.ds(at, step)), half + at, width - half - at)


def projection(queries, earlier, cum, pre, weight, taps, deep):
    frames, width, tokens = queries.shape
    rows = (HALO + frames) * tokens
    depth = weight.shape[1] * weight.shape[2]
    whole = pl.BlockSpec(memory_space=pltpu.VMEM)
    anywhere = pl.BlockSpec(memory_space=pl.ANY)
    return pl.pallas_call(
        functools.partial(project, deep),
        out_shape=jax.ShapeDtypeStruct(queries.shape, queries.dtype),
        in_specs=[anywhere] * 5 + [whole],
        out_specs=whole,
        scratch_shapes=[pltpu.VMEM(ref.shape, ref.dtype) for ref in (queries, earlier, cum, pre, weight)] + [
            pltpu.VMEM((depth, tokens), jnp.bfloat16),
            pltpu.VMEM((rows, depth), jnp.bfloat16),
            pltpu.SemaphoreType.DMA((6,)),
        ],
        cost_estimate=pl.CostEstimate(
            flops=2 * rows * depth * width, bytes_accessed=2 * depth * width, transcendentals=0),
        compiler_params=pltpu.CompilerParams(vmem_limit_bytes=50 * 2**20),
    )(queries, earlier, cum, pre, weight, taps)


def up_to(value, multiple):
    return -(-value // multiple) * multiple


def per_device(sections, lanes, queries, keys, values, out_weight, conv_taps):
    width = queries.shape[2]
    lanes_y, outer = lanes // 2, sections // 2
    queries, keys, values = (jnp.swapaxes(a, 1, 2) for a in (queries, keys, values))
    tall = up_to(HEADS * LANES, 16 * lanes) // lanes
    deep = out_weight.shape[0]
    shift = max(n * deep % 16 for n in range(sections))
    deep_pad = up_to(deep + shift, 16 * lanes_y)
    wide = up_to(width, 2 * LANES)
    weight = lax.dynamic_update_slice(
        jnp.zeros((deep_pad, wide), out_weight.dtype), out_weight,
        (lax.rem(lax.axis_index("frame") * deep, 16), 0))
    weight = weight.reshape(deep_pad, 2, wide // 2).transpose(1, 0, 2)
    cum, pre, weight, earlier = exchanged(keys, values, weight, queries, tall, outer, lanes_y)
    mixed = projection(queries, earlier, cum, pre, weight, conv_taps, deep)
    return jnp.swapaxes(mixed, 1, 2)


def solution(mesh):
    split = P("frame", "space", None)
    return jax.shard_map(
        functools.partial(per_device, mesh.shape["frame"], mesh.shape["space"]), mesh=mesh,
        in_specs=(split, split, split, P("frame", None), P()), out_specs=split, check_vma=False)
```

time: 162 us -> 136 us (0.84)
  the two profiles are of different devices: /device:TPU:31 before, /device:TPU:25 now
where the time goes in v3:
time: 136 us; the launch traced here: 135 us
  Pallas kernels  118 us (87%)
  local copies, waits for them, and re-layouts  17.7 us (13%)
    pallas_call x1, Pallas kernels, exchanged(): pl.pallas_call(functools.partial(exchange, outer, lanes_y), out_shape=(ja...  101 us
    pallas_call x1, Pallas kernels, projection(): pl.pallas_call(functools.partial(project, deep), out_shape=jax.ShapeDtype...  16.9 us
    dynamic_update_slice x1, local copies, waits for them, and re-layouts, per_device(): lax.dynamic_update_slice(jnp.zeros((deep_pad, wide), out_weight.dtype), o...  11.4 us
    unnamed x10, local copies, waits for them, and re-layouts  3.66 us

profile of v3, /device:TPU:25, one launch (start us, length us, event | category | flops | bytes accessed | tf_op | source)
XLA Modules:
  0.0 135.3 jit_solution(6639140571409286169)
XLA Ops:
  0.0 1.1 broadcast_in_dim.3
  1.1 0.0 copy-start
  1.2 11.4 %dynamic_update_slice.3 = bf16[288,2304]{1,0:T(8,128)(2,1)} dynamic-update-slice(bf16[288,2304]{1,0:T(8,128)(2,1)} %broadcast_in_dim.3, bf16[280,2240]{1,0:T(8,128)(2,1)} %param.8, s32[]{:T(128)S(6)} %select_n.3, s32[]{:T(128)} %constant.15.clone.1) | dynamic-update-slice | bytes 2508804 | tf_op jit(solution)/shard_map/dynamic_update_slice | solution.py:491
  12.5 0.0 copy-start.1
  12.5 1.6 %copy.9 = bf16[36,2,8,1152]{3,2,0,1:T(8,128)(2,1)S(1)} copy(bf16[36,2,8,1152]{3,2,1,0:T(8,128)(2,1)} %bitcast.16) | data formatting | bytes 2654208 | tf_op jit(solution)/shard_map/reshape | solution.py:494
  14.1 0.0 copy-done
  14.1 0.5 copy-done.1
  14.6 0.0 copy-start.2
  14.6 1.6 %copy-done.2 = bf16[4,128,2240]{1,2,0:T(8,128)(2,1)S(1)} copy-done((bf16[4,128,2240]{1,2,0:T(8,128)(2,1)S(1)}, bf16[4,128,2240]{1,2,0:T(8,128)(2,1)}, u32[]{:S(2)}) %copy-start.2) | copy-done | bytes 2293784
  16.2 0.0 copy-start.4
  16.2 100.6 %shard_map.55 = (bf16[2,2,4,640,128]{4,3,2,1,0:T(8,128)(2,1)S(1)}, bf16[2,2,2,640,128]{4,3,2,1,0:T(8,128)(2,1)S(1)}, bf16[2,8,288,1152]{3,2,1,0:T(8,128)(2,1)}, bf16[2,2240,128]{2,1,0:T(8,128)(2,1)S(1)}) custom-call(bf16[4,2240,128]{2,1,0:T(8,128)(2,1)S(1)} %bitcast.12, bf16[4,2240,128]{2,1,0:T(8,128)(2,1)S(1)} %bitcast.13, ...), custom_call_target="tpu_custom_call" | custom-call | tf_op jit(solution)/shard_map/pallas_call | solution.py:316
  116.9 0.0 copy-start.3
  116.9 1.5 %copy-done.3 = bf16[2,2,4,640,128]{4,3,2,1,0:T(8,128)(2,1)} copy-done((bf16[2,2,4,640,128]{4,3,2,1,0:T(8,128)(2,1)}, bf16[2,2,4,640,128]{4,3,2,1,0:T(8,128)(2,1)S(1)}, u32[]{:S(2)}) %copy-start.3) | copy-done | bytes 2621464
  118.4 0.0 copy-done.4
  118.4 16.9 %shard_map.56 = bf16[4,2240,128]{2,1,0:T(8,128)(2,1)} custom-call(bf16[4,2240,128]{2,1,0:T(8,128)(2,1)} %bitcast.14, bf16[2,2240,128]{2,1,0:T(8,128)(2,1)S(1)} %get-tuple-element.9.early_hbm, bf16[2,2,4,640,128]{4,3,2,1,0:T(8,128)(2,1)} %copy-done.3, bf16[2,2,2,640,128]{4,3,2,1,0:T(8,128)(2,1)S(1)} %get-tuple-element.11.pre_hbm, ...), custom_call_target="tpu_custom_call" | custom-call | flops 7927234560 | bytes 10321920 | tf_op jit(solution)/shard_map/pallas_call | solution.py:462
Async XLA Ops:
  1.1 12.9 %copy-start = (bf16[4,128,2240]{1,2,0:T(8,128)(2,1)S(1)}, bf16[4,128,2240]{1,2,0:T(8,128)(2,1)}, u32[]{:S(2)}) copy-start(bf16[4,128,2240]{1,2,0:T(8,128)(2,1)} %param.6) | copy-start | bytes 6881284
  12.5 2.0 %copy-start.1 = (bf16[4,128,2240]{1,2,0:T(8,128)(2,1)S(1)}, bf16[4,128,2240]{1,2,0:T(8,128)(2,1)}, u32[]{:S(2)}) copy-start(bf16[4,128,2240]{1,2,0:T(8,128)(2,1)} %param.7) | copy-start | bytes 6881284
  14.6 1.6 %copy-start.2 = (bf16[4,128,2240]{1,2,0:T(8,128)(2,1)S(1)}, bf16[4,128,2240]{1,2,0:T(8,128)(2,1)}, u32[]{:S(2)}) copy-start(bf16[4,128,2240]{1,2,0:T(8,128)(2,1)} %param.5) | copy-start | bytes 6881284
  16.2 102.2 %copy-start.4 = (f32[3,2240]{1,0:T(4,128)S(1)}, f32[3,2240]{1,0:T(4,128)}, u32[]{:S(2)}) copy-start(f32[3,2240]{1,0:T(4,128)} %taps_ref.1) | copy-start | bytes 80644
  116.9 1.6 %copy-start.3 = (bf16[2,2,4,640,128]{4,3,2,1,0:T(8,128)(2,1)}, bf16[2,2,4,640,128]{4,3,2,1,0:T(8,128)(2,1)S(1)}, u32[]{:S(2)}) copy-start(bf16[2,2,4,640,128]{4,3,2,1,0:T(8,128)(2,1)S(1)} %get-tuple-element.10.cum_hbm) | copy-start | bytes 7864324

commit v4 on v3

--- a/solution.py
+++ b/solution.py
@@ -22,8 +22,8 @@
         start = end
 
 
-def exchange(outer, lanes_y, k_in, v_in, w_in, q_in, cum_out, pre_out, w_out, q_out,
-             kv_in, sib_kv, chip_kv, y_kv, frame_kv, cum, pre, x_got, pair_msg, edge_msg, pair_got, edge_got,
+def exchange(outer, lanes_y, k_hbm, v_hbm, w_hbm, q_in, cum_out, pre_out, w_out, q_out,
+             k_in, v_in, w_own, w_in, kv_in, sib_kv, chip_kv, y_kv, frame_kv, cum, pre, x_got, pair_msg, edge_msg, pair_got, edge_got,
              own_sem, kv_sem, z_sem, x_sem, y_sem, sz_sem, sx_sem, sy_sem, p_sem):
     frame = lax.axis_index("frame")
     space = lax.axis_index("space")
@@ -56,6 +56,11 @@
 
     def y_from(d):
         return lax.rem(y + lanes_y - d, lanes_y)
+
+    incoming = [pltpu.make_async_copy(src, dst, own_sem.at[3 + n])
+                for n, (src, dst) in enumerate(((w_hbm, w_own), (k_hbm, k_in), (v_hbm, v_in)))]
+    for load in incoming:
+        load.start()
 
     barrier = pltpu.get_barrier_semaphore()
 
@@ -72,6 +77,16 @@
     onto = jnp.logical_and(i == 1, o < outer - 1)
     when(into, lambda: greet(at(o_=o - 1, i_=1)))
     when(onto, lambda: greet(at(o_=o + 1, i_=0)))
+    deep, width = w_own.shape
+    half = w_in.shape[2]
+    w_in[...] = jnp.zeros(w_in.shape, jnp.bfloat16)
+    incoming[0].wait()
+    for shift in sorted({n * deep % 16 for n in range(2 * outer)}):
+        def lay(shift=shift):
+            w_in[0, shift:shift + deep, :] = w_own[:, :half]
+            w_in[1, shift:shift + deep, :width - half] = w_own[:, half:]
+        pl.when(lax.rem(frame * deep, 16) == shift)(lay)
+
     peers = (outer - 1) + (lanes_y - 1) + 2
     pl.semaphore_wait(barrier, peers + jnp.where(jnp.logical_or(into, onto), 1, 0))
 
@@ -167,6 +182,9 @@
     def halo(f):
         launch(frame < 2 * outer - 1,
                lambda: copy(q_in.at[frames - HALO + f], q_out.at[f], p_sem.at[f], (frame + 1, space)))
+
+    for load in incoming[1:]:
+        load.wait()
 
     tokens = k_in.shape[2]
     gap = LANES - HEAD_DIM
@@ -305,25 +323,28 @@
         when(cond, lambda make=make: make().wait_send())
 
 
-def exchanged(keys, values, weight, queries, tall, outer, lanes_y):
+def exchanged(keys, values, weight, queries, padded, tall, outer, lanes_y):
     frames = keys.shape[0]
     count = 2 * outer - 1
     tile = (tall, LANES)
     half = jnp.bfloat16
     dma = pltpu.SemaphoreType.DMA
-    whole = pl.BlockSpec(memory_space=pltpu.VMEM)
     anywhere = pl.BlockSpec(memory_space=pl.ANY)
     return pl.pallas_call(
         functools.partial(exchange, outer, lanes_y),
         out_shape=(
             jax.ShapeDtypeStruct((2, lanes_y, frames) + tile, half),
             jax.ShapeDtypeStruct((2, lanes_y, HALO) + tile, half),
-            jax.ShapeDtypeStruct((2, 2 * outer) + weight.shape[1:], half),
+            jax.ShapeDtypeStruct((2, 2 * outer) + padded, half),
             jax.ShapeDtypeStruct((HALO,) + queries.shape[1:], half),
         ),
-        in_specs=[whole, whole, anywhere, anywhere],
+        in_specs=[anywhere] * 4,
         out_specs=(anywhere,) * 4,
         scratch_shapes=[
+            pltpu.VMEM(keys.shape, half),
+            pltpu.VMEM(values.shape, half),
+            pltpu.VMEM(weight.shape, half),
+            pltpu.VMEM((2,) + padded, half),
             pltpu.VMEM((2, lanes_y, frames) + tile, half),
             pltpu.VMEM((lanes_y, frames) + tile, half),
             pltpu.VMEM((lanes_y, frames) + tile, half),
@@ -336,7 +357,7 @@
             pltpu.VMEM(tile, half),
             pltpu.VMEM((outer,) + tile, half),
             pltpu.VMEM(tile, half),
-            dma((3,)),
+            dma((6,)),
             dma((3 + 3 * lanes_y, 2)),
             dma((2, outer, 2)),
             dma((count, 2)),
@@ -347,7 +368,7 @@
             dma((HALO + 1 + outer, 2)),
         ],
         compiler_params=pltpu.CompilerParams(
-            collective_id=0, has_side_effects=True, vmem_limit_bytes=40 * 2**20),
+            collective_id=0, has_side_effects=True, vmem_limit_bytes=56 * 2**20),
     )(keys, values, weight, queries)
 
 
@@ -471,7 +492,7 @@
         ],
         cost_estimate=pl.CostEstimate(
             flops=2 * rows * depth * width, bytes_accessed=2 * depth * width, transcendentals=0),
-        compiler_params=pltpu.CompilerParams(vmem_limit_bytes=50 * 2**20),
+        compiler_params=pltpu.CompilerParams(vmem_limit_bytes=58 * 2**20),
     )(queries, earlier, cum, pre, weight, taps)
 
 
@@ -486,13 +507,9 @@
     tall = up_to(HEADS * LANES, 16 * lanes) // lanes
     deep = out_weight.shape[0]
     shift = max(n * deep % 16 for n in range(sections))
-    deep_pad = up_to(deep + shift, 16 * lanes_y)
-    wide = up_to(width, 2 * LANES)
-    weight = lax.dynamic_update_slice(
-        jnp.zeros((deep_pad, wide), out_weight.dtype), out_weight,
-        (lax.rem(lax.axis_index("frame") * deep, 16), 0))
-    weight = weight.reshape(deep_pad, 2, wide // 2).transpose(1, 0, 2)
-    cum, pre, weight, earlier = exchanged(keys, values, weight, queries, tall, outer, lanes_y)
+    padded = (up_to(deep + shift, 16 * lanes_y), up_to(width, 2 * LANES) // 2)
+    cum, pre, weight, earlier = exchanged(
+        keys, values, out_weight, queries, padded, tall, outer, lanes_y)
     mixed = projection(queries, earlier, cum, pre, weight, conv_taps, deep)
     return jnp.swapaxes(mixed, 1, 2)
 

time: 136 us -> 119 us (0.88)
  local copies, waits for them, and re-layouts: 17.7 us -> 0 us
    dynamic_update_slice x1 -> x0, local copies, waits for them, and re-layouts: 11.4 us -> none  [per_device(): lax.dynamic_update_slice(jnp.zeros((deep_pad, wide), out_weight.dtype), o...]
    unnamed x10 -> x0, local copies, waits for them, and re-layouts: 3.66 us -> none
    reshape x1 -> x0, local copies, waits for them, and re-layouts: 1.57 us -> none  [per_device(): weight = weight.reshape(deep_pad, 2, wide // 2).transpose(1, 0, 2)]
    pallas_call x1, Pallas kernels: 16.9 us -> 18.4 us  [projection(): pl.pallas_call(functools.partial(project, deep), out_shape=jax.ShapeDtype...]
where the time goes in v4:
time: 119 us
  Pallas kernels  119 us (100%)
    pallas_call x1, Pallas kernels, exchanged(): pl.pallas_call(functools.partial(exchange, outer, lanes_y), out_shape=(ja...  101 us
    pallas_call x1, Pallas kernels, projection(): pl.pallas_call(functools.partial(project, deep), out_shape=jax.ShapeDtype...  18.4 us

profile of v4, /device:TPU:25, one launch (start us, length us, event | category | flops | bytes accessed | tf_op | source)
XLA Modules:
  0.0 119.1 jit_solution(16602497652446929117)
XLA Ops:
  0.0 100.7 %shard_map.55 = (bf16[2,2,4,640,128]{4,3,2,1,0:T(8,128)(2,1)}, bf16[2,2,2,640,128]{4,3,2,1,0:T(8,128)(2,1)}, bf16[2,8,288,1152]{3,2,1,0:T(8,128)(2,1)}, bf16[2,2240,128]{2,1,0:T(8,128)(2,1)}) custom-call(bf16[4,2240,128]{2,1,0:T(8,128)(2,1)} %bitcast.4, bf16[4,2240,128]{2,1,0:T(8,128)(2,1)} %bitcast.5, bf16[280,2240]{1,0:T(8,128)(2,1)} %w_hbm.1, ...), custom_call_target="tpu_custom_call" | custom-call | tf_op jit(solution)/shard_map/pallas_call | solution.py:333
  100.7 18.4 %shard_map.56 = bf16[4,2240,128]{2,1,0:T(8,128)(2,1)} custom-call(bf16[4,2240,128]{2,1,0:T(8,128)(2,1)} %bitcast.7, bf16[2,2240,128]{2,1,0:T(8,128)(2,1)} %get-tuple-element.9.early_hbm, bf16[2,2,4,640,128]{4,3,2,1,0:T(8,128)(2,1)} %get-tuple-element.10.cum_hbm, bf16[2,2,2,640,128]{4,3,2,1,0:T(8,128)(2,1)} %get-tuple-element.11.pre_hbm, ...), custom_call_target="tpu_custom_call" | custom-call | flops 7927234560 | bytes 10321920 | tf_op jit(solution)/shard_map/pallas_call | solution.py:483

commit v5 on v4

--- a/solution.py
+++ b/solution.py
@@ -23,7 +23,7 @@
 
 
 def exchange(outer, lanes_y, k_hbm, v_hbm, w_hbm, q_in, cum_out, pre_out, w_out, q_out,
-             k_in, v_in, w_own, w_in, kv_in, sib_kv, chip_kv, y_kv, frame_kv, cum, pre, x_got, pair_msg, edge_msg, pair_got, edge_got,
+             k_in, v_in, w_own, w_in, kv_in, sib_kv, chip_kv, y_kv, frame_kv, cum, pre, x_got, pair_msg, edge_msg, pair_got, edge_got, relay,
              own_sem, kv_sem, z_sem, x_sem, y_sem, sz_sem, sx_sem, sy_sem, p_sem):
     frame = lax.axis_index("frame")
     space = lax.axis_index("space")
@@ -73,10 +73,6 @@
         greet(at(y_=y_far(d)))
     greet(at(i_=1 - i))
     greet(at(c_=1 - c))
-    into = jnp.logical_and(i == 0, o > 0)
-    onto = jnp.logical_and(i == 1, o < outer - 1)
-    when(into, lambda: greet(at(o_=o - 1, i_=1)))
-    when(onto, lambda: greet(at(o_=o + 1, i_=0)))
     deep, width = w_own.shape
     half = w_in.shape[2]
     w_in[...] = jnp.zeros(w_in.shape, jnp.bfloat16)
@@ -88,7 +84,7 @@
         pl.when(lax.rem(frame * deep, 16) == shift)(lay)
 
     peers = (outer - 1) + (lanes_y - 1) + 2
-    pl.semaphore_wait(barrier, peers + jnp.where(jnp.logical_or(into, onto), 1, 0))
+    pl.semaphore_wait(barrier, peers)
 
     def source(key):
         t = (key + 1) // 2
@@ -179,9 +175,24 @@
     locals_ = [pltpu.make_async_copy(w_in, w_out.at[:, frame], own_sem.at[0])]
     locals_[0].start()
 
-    def halo(f):
-        launch(frame < 2 * outer - 1,
-               lambda: copy(q_in.at[frames - HALO + f], q_out.at[f], p_sem.at[f], (frame + 1, space)))
+    via = HALO + 1 + outer
+    onward = jnp.logical_and(i == 1, o < outer - 1)
+    last = frames - HALO
+
+    def halo_pair(f):
+        launch(i == 0, lambda: copy(q_in.at[last + f], q_out.at[f], p_sem.at[f], at(i_=1)))
+
+    def halo_onward():
+        launch(onward, lambda: copy(q_in.at[last], relay, p_sem.at[via], at(i_=0)))
+        launch(onward, lambda: copy(q_in.at[last + 1], relay, p_sem.at[via + 1], at(o_=o + 1)))
+
+    def halo_pass():
+        lower = jnp.logical_and(i == 0, o < outer - 1)
+        upper = jnp.logical_and(i == 1, o > 0)
+        when(lower, lambda: copy(relay, relay, p_sem.at[via], at(c_=1 - c)).wait_recv())
+        launch(lower, lambda: copy(relay, q_out.at[0], p_sem.at[via + 2], at(o_=o + 1)))
+        when(upper, lambda: copy(relay, relay, p_sem.at[via + 1], at(c_=1 - c)).wait_recv())
+        launch(upper, lambda: copy(relay, q_out.at[1], p_sem.at[via + 3], at(i_=0)))
 
     for load in incoming[1:]:
         load.wait()
@@ -215,7 +226,8 @@
         if d:
             launch(True, lambda d=d: copy(chip_kv.at[y_far(d)], y_kv.at[d], kv_sem.at[3 + d],
                                           at(y_=y_far(d))))
-    halo(0)
+    halo_pair(0)
+    halo_onward()
     z_wait(1)
     if outer > 2:
         z_send(2)
@@ -289,14 +301,16 @@
             sib_z(key)
         if t == 2:
             pair()
-            halo(1)
+            halo_pair(1)
+            halo_pass()
         for key in (2 * t - 3, 2 * t - 2):
             x_pass(key)
         for key in ((0,) if t == 2 else (2 * t - 5, 2 * t - 4)):
             y_pass(key)
     if outer <= 2:
         pair()
-        halo(1)
+        halo_pair(1)
+        halo_pass()
         y_pass(0)
     prefix()
     if outer > 2:
@@ -313,8 +327,10 @@
         other = out.at[1 - c]
         copy(other, other, sems, at(c_=1 - c)).wait_recv()
     for f in range(HALO):
-        ref = q_out.at[f]
-        when(frame > 0, lambda f=f, ref=ref: copy(ref, ref, p_sem.at[f], at(c_=1 - c)).wait_recv())
+        def landed(sems, f):
+            copy(q_out.at[f], q_out.at[f], sems, at(c_=1 - c)).wait_recv()
+        when(i == 1, lambda f=f: landed(p_sem.at[f], f))
+        when(jnp.logical_and(i == 0, o > 0), lambda f=f: landed(p_sem.at[via + 2 + f], f))
     for key in keys:
         sib_wait(key)
     locals_[0].wait()
@@ -357,6 +373,7 @@
             pltpu.VMEM(tile, half),
             pltpu.VMEM((outer,) + tile, half),
             pltpu.VMEM(tile, half),
+            pltpu.VMEM(queries.shape[1:], half),
             dma((6,)),
             dma((3 + 3 * lanes_y, 2)),
             dma((2, outer, 2)),
@@ -365,7 +382,7 @@
             dma((count, 2)),
             dma((count, 2)),
             dma((count, lanes_y, 2)),
-            dma((HALO + 1 + outer, 2)),
+            dma((HALO + 5 + outer, 2)),
         ],
         compiler_params=pltpu.CompilerParams(
             collective_id=0, has_side_effects=True, vmem_limit_bytes=56 * 2**20),

time: 119 us -> 115 us (0.966)
  the two profiles are of different devices: /device:TPU:25 before, /device:TPU:31 now
where the time goes in v5:
time: 115 us; the launch traced here: 114 us
  Pallas kernels  114 us (99%)
    pallas_call x1, Pallas kernels, exchanged(): pl.pallas_call(functools.partial(exchange, outer, lanes_y), out_shape=(ja...  95.4 us
    pallas_call x1, Pallas kernels, projection(): pl.pallas_call(functools.partial(project, deep), out_shape=jax.ShapeDtype...  18.4 us

profile of v5, /device:TPU:31, one launch (start us, length us, event | category | flops | bytes accessed | tf_op | source)
XLA Modules:
  0.0 113.8 jit_solution(7362739244224034625)
XLA Ops:
  0.0 95.4 %shard_map.55 = (bf16[2,2,4,640,128]{4,3,2,1,0:T(8,128)(2,1)}, bf16[2,2,2,640,128]{4,3,2,1,0:T(8,128)(2,1)}, bf16[2,8,288,1152]{3,2,1,0:T(8,128)(2,1)}, bf16[2,2240,128]{2,1,0:T(8,128)(2,1)}) custom-call(bf16[4,2240,128]{2,1,0:T(8,128)(2,1)} %bitcast.4, bf16[4,2240,128]{2,1,0:T(8,128)(2,1)} %bitcast.5, bf16[280,2240]{1,0:T(8,128)(2,1)} %w_hbm.1, ...), custom_call_target="tpu_custom_call" | custom-call | tf_op jit(solution)/shard_map/pallas_call | solution.py:349
  95.4 18.4 %shard_map.56 = bf16[4,2240,128]{2,1,0:T(8,128)(2,1)} custom-call(bf16[4,2240,128]{2,1,0:T(8,128)(2,1)} %bitcast.7, bf16[2,2240,128]{2,1,0:T(8,128)(2,1)} %get-tuple-element.9.early_hbm, bf16[2,2,4,640,128]{4,3,2,1,0:T(8,128)(2,1)} %get-tuple-element.10.cum_hbm, bf16[2,2,2,640,128]{4,3,2,1,0:T(8,128)(2,1)} %get-tuple-element.11.pre_hbm, ...), custom_call_target="tpu_custom_call" | custom-call | flops 7927234560 | bytes 10321920 | tf_op jit(solution)/shard_map/pallas_call | solution.py:500

commit v6 on v5

--- a/solution.py
+++ b/solution.py
@@ -261,13 +261,13 @@
         for d in range(1, outer):
             launch(o + d < outer,
                    lambda d=d: copy(pair_msg, pair_got.at[d], p_sem.at[HALO + 1 + d], at(o_=o + d)))
-        launch(o + 1 < outer, lambda: copy(edge_msg, edge_got, p_sem.at[HALO + 1], at(o_=o + 1)))
+        launch(jnp.logical_and(i == 0, o + 1 < outer), lambda: copy(edge_msg, edge_got, p_sem.at[HALO + 1], at(o_=o + 1)))
 
     def prefix():
         for d in range(1, outer):
             when(o >= d, lambda d=d: copy(pair_msg, pair_got.at[d], p_sem.at[HALO + 1 + d],
                                           at(c_=1 - c)).wait_recv())
-        when(o >= 1, lambda: copy(edge_msg, edge_got, p_sem.at[HALO + 1], at(c_=1 - c)).wait_recv())
+        when(jnp.logical_and(i == 0, o >= 1), lambda: copy(edge_msg, edge_got, p_sem.at[HALO + 1], at(c_=1 - c)).wait_recv())
         zero = jnp.zeros(pair_msg.shape, jnp.float32)
         far = zero
         for d in range(2, outer):
@@ -302,9 +302,10 @@
         if t == 2:
             pair()
             halo_pair(1)
-            halo_pass()
         for key in (2 * t - 3, 2 * t - 2):
             x_pass(key)
+        if t == 2:
+            halo_pass()
         for key in ((0,) if t == 2 else (2 * t - 5, 2 * t - 4)):
             y_pass(key)
     if outer <= 2:

time: 115 us -> 114 us (level)
  Pallas kernels: 114 us -> 112 us
    pallas_call x1, Pallas kernels: 95.4 us -> 93.9 us  [exchanged(): pl.pallas_call(functools.partial(exchange, outer, lanes_y), out_shape=(ja...]
where the time goes in v6:
time: 114 us; the launch traced here: 112 us
  Pallas kernels  112 us (98%)
    pallas_call x1, Pallas kernels, exchanged(): pl.pallas_call(functools.partial(exchange, outer, lanes_y), out_shape=(ja...  93.9 us
    pallas_call x1, Pallas kernels, projection(): pl.pallas_call(functools.partial(project, deep), out_shape=jax.ShapeDtype...  18.4 us

profile of v6, /device:TPU:31, one launch (start us, length us, event | category | flops | bytes accessed | tf_op | source)
XLA Modules:
  0.0 112.3 jit_solution(1384337180403436584)
XLA Ops:
  0.0 93.9 %shard_map.55 = (bf16[2,2,4,640,128]{4,3,2,1,0:T(8,128)(2,1)}, bf16[2,2,2,640,128]{4,3,2,1,0:T(8,128)(2,1)}, bf16[2,8,288,1152]{3,2,1,0:T(8,128)(2,1)}, bf16[2,2240,128]{2,1,0:T(8,128)(2,1)}) custom-call(bf16[4,2240,128]{2,1,0:T(8,128)(2,1)} %bitcast.4, bf16[4,2240,128]{2,1,0:T(8,128)(2,1)} %bitcast.5, bf16[280,2240]{1,0:T(8,128)(2,1)} %w_hbm.1, ...), custom_call_target="tpu_custom_call" | custom-call | tf_op jit(solution)/shard_map/pallas_call | solution.py:350
  93.9 18.4 %shard_map.56 = bf16[4,2240,128]{2,1,0:T(8,128)(2,1)} custom-call(bf16[4,2240,128]{2,1,0:T(8,128)(2,1)} %bitcast.7, bf16[2,2240,128]{2,1,0:T(8,128)(2,1)} %get-tuple-element.9.early_hbm, bf16[2,2,4,640,128]{4,3,2,1,0:T(8,128)(2,1)} %get-tuple-element.10.cum_hbm, bf16[2,2,2,640,128]{4,3,2,1,0:T(8,128)(2,1)} %get-tuple-element.11.pre_hbm, ...), custom_call_target="tpu_custom_call" | custom-call | flops 7927234560 | bytes 10321920 | tf_op jit(solution)/shard_map/pallas_call | solution.py:501
